TPU v7x, 256 devices: a whole 4x4x8 slice. The times are simulated.
256 devices in a mesh: gx: 16 (over y_lo, x, core), gy: 8 (over z), gz: 2 (over y_hi).
Axes of the slice: x: 4, y: 4 (y_hi: 2, y_lo: 2; y = y_hi * 2 + y_lo), z: 8, core: 2. Of those that a mesh axis runs over, the one named last changes fastest.
Arguments:
- e_field: float32 [3, 128, 128, 256], P(None, 'gx', 'gy', 'gz'), may hold values from -6 to 6
- h_field: float32 [3, 128, 128, 256], P(None, 'gx', 'gy', 'gz'), may hold values from -6 to 6
- permittivity: float32 [128, 128, 256], P('gx', 'gy', 'gz'), may hold values from 1 to 4
- wall_mask: int32 [128, 128, 256], P('gx', 'gy', 'gz'), may hold values 0 or 1
- poles: float32 [8, 3, 128, 128, 256], P(None, None, 'gx', 'gy', 'gz'), may hold values from -4 to 4
- pole_decay: float32 [8], replicated, may hold values from 0.2 to 0.95
- pole_gain: float32 [8], replicated, may hold values from 0.05 to 0.3
- face_cells: int32 [8192], P(('gx', 'gy', 'gz')), may hold values from 0 to 16383
- owners: int32 [8192, 1], P(('gx', 'gy', 'gz')), may hold values from 0 to 15; in each aligned block of 32 rows (0 to 31, 32 to 63, ...) at most 4 rows name the same one
- history: bfloat16 [63, 4, 8192], P(None, None, ('gx', 'gy', 'gz')), may hold values from -6 to 6
- steering: bfloat16 [4, 16384, 4096], P(None, ('gx', 'gy'), 'gz'), may hold values from -0.03125 to 0.03125
Outputs:
- e_next: float32 [3, 128, 128, 256], P(None, 'gx', 'gy', 'gz')
- h_next: float32 [3, 128, 128, 256], P(None, 'gx', 'gy', 'gz')
- poles_next: float32 [8, 3, 128, 128, 256], P(None, None, 'gx', 'gy', 'gz')
- far_field: float32 [2, 256, 4096], P(None, ('gx', 'gy'), 'gz')
Inputs may be any that keep to these rules, and one draw needn't show every extreme that they name: `face_cells`: index of the sample's cell within its device's block, row-major over 8 x 16 x 128. `owners`: among the samples of one device at most 4 name the same owner, and some device has exactly 4 for one owner.
All inputs are finite; a program needn't handle non-finite values. No bound on the sum of `wall_mask` on one device may be relied on, other than what follows from the above.
Results may differ from a plain program's by a relative error of at most 0.00063.
Values may be sent and summed in bfloat16 or wider, within the bound.
No kernel may reach another device: no remote copies, remote signals or barrier semaphores. Data moves between devices by JAX's collectives and lax.ppermute only.
A program may use at most 64 MiB of HBM per device.

v0:
```python
import math

import jax
import jax.numpy as jnp
from jax import lax
from jax.sharding import PartitionSpec as P

FREQS = 256


def padded_2(block, sides, width):
    for axis, dim in sides:
        count = lax.axis_size(axis)
        forward = [(i, i + 1) for i in range(count - 1)]
        backward = [(target, source) for source, target in forward]
        low = lax.ppermute(
            lax.slice_in_dim(block, block.shape[dim] - width, None, axis=dim), axis, forward
        )
        high = lax.ppermute(lax.slice_in_dim(block, 0, width, axis=dim), axis, backward)
        block = jnp.concatenate([low, block, high], axis=dim)
    return block


def window(field, shift_x, shift_y, shift_z, span_x, span_y, span_z):
    return lax.slice(
        field, (shift_x, shift_y, shift_z), (shift_x + span_x, shift_y + span_y, shift_z + span_z)
    )


def spectral_rows(count, freqs, steps):
    times = jnp.arange(steps, dtype=jnp.float32)
    levels = jnp.arange(count, dtype=jnp.float32) + 0.5
    phase = math.pi / (2.0 * freqs) * levels[:, None] * times[None, :]
    scale = 1.0 / math.sqrt(steps)
    return jnp.stack([jnp.cos(phase) * scale, -jnp.sin(phase) * scale])


def bucket_rank(owner, groups):
    onehot = (owner[..., None] == jnp.arange(groups, dtype=jnp.int32)).astype(jnp.int32)
    return jnp.sum((jnp.cumsum(onehot, axis=-2) - onehot) * onehot, axis=-1)


def project(tile_rows, weights, steps):
    currents = tile_rows.reshape(tile_rows.shape[0], steps, 4)
    return jnp.einsum("rtc,crd->td", currents, weights, preferred_element_type=jnp.float32)


def fields_both(e_field, h_field):
    span_x, span_y, span_z = (e_field.shape[1], e_field.shape[2], e_field.shape[3])
    both = jnp.concatenate([e_field, h_field], axis=0)
    padded = padded_2(both, (("gx", 1), ("gy", 2), ("gz", 3)), 1)
    ext_x, ext_y, ext_z = (span_x + 1, span_y + 1, span_z + 1)

    def upper(comp, shift_x, shift_y, shift_z):
        return window(padded[comp], shift_x, shift_y, shift_z, ext_x, ext_y, ext_z)

    mag_x = upper(3, 0, 0, 0) - 0.5 * (
        upper(2, 0, 1, 0) - upper(2, 0, 0, 0) - (upper(1, 0, 0, 1) - upper(1, 0, 0, 0))
    )
    mag_y = upper(4, 0, 0, 0) - 0.5 * (
        upper(0, 0, 0, 1) - upper(0, 0, 0, 0) - (upper(2, 1, 0, 0) - upper(2, 0, 0, 0))
    )
    mag_z = upper(5, 0, 0, 0) - 0.5 * (
        upper(1, 1, 0, 0) - upper(1, 0, 0, 0) - (upper(0, 0, 1, 0) - upper(0, 0, 0, 0))
    )
    keep_x = (jnp.arange(ext_x) > 0) | (lax.axis_index("gx") > 0)
    keep_y = (jnp.arange(ext_y) > 0) | (lax.axis_index("gy") > 0)
    keep_z = (jnp.arange(ext_z) > 0) | (lax.axis_index("gz") > 0)
    keep = keep_x[:, None, None] & keep_y[None, :, None] & keep_z[None, None, :]
    magnetic = jnp.where(keep[None], jnp.stack([mag_x, mag_y, mag_z]), 0.0)

    def lower(comp, back_x, back_y, back_z):
        return window(magnetic[comp], 1 - back_x, 1 - back_y, 1 - back_z, span_x, span_y, span_z)

    drive = jnp.stack(
        [
            lower(2, 0, 0, 0) - lower(2, 0, 1, 0) - (lower(1, 0, 0, 0) - lower(1, 0, 0, 1)),
            lower(0, 0, 0, 0) - lower(0, 0, 0, 1) - (lower(2, 0, 0, 0) - lower(2, 1, 0, 0)),
            lower(1, 0, 0, 0) - lower(1, 1, 0, 0) - (lower(0, 0, 0, 0) - lower(0, 0, 1, 0)),
        ]
    )
    return (magnetic[:, 1:, 1:, 1:], drive)


def per_device(
    e_field,
    h_field,
    permittivity,
    wall_mask,
    poles,
    pole_decay,
    pole_gain,
    face_cells,
    owners,
    history,
    steering,
):
    h_next, drive = fields_both(e_field, h_field)
    poles_next = (
        pole_decay[:, None, None, None, None] * poles
        + pole_gain[:, None, None, None, None] * drive[None]
    )
    e_next = jnp.where(
        wall_mask[None] == 1,
        jnp.sum(poles_next, axis=0),
        e_field + (0.5 / permittivity)[None] * drive,
    )
    count = face_cells.shape[0]
    steps = history.shape[0] + 1
    picked = jnp.stack([e_next[0], e_next[1], h_next[0], h_next[1]]).reshape(4, -1)
    fresh = jnp.take(picked, face_cells, axis=1).astype(jnp.bfloat16)
    series = jnp.concatenate([history, fresh[None]], axis=0)
    sample_rows = jnp.transpose(series, (2, 0, 1)).reshape(count, steps * 4)
    owner = owners[:, 0]
    groups = lax.axis_size("gx")
    depth = lax.axis_size("gz")
    capacity = 2 * count // groups
    tile = steering.shape[1]
    every_rows, every_owner = (
        lax.all_gather(sample_rows, ("gx", "gz"), axis=0, tiled=True),
        lax.all_gather(owner[:, None], ("gx", "gz"), axis=0, tiled=True),
    )
    owner_all = every_owner[:, 0].reshape(groups * depth, count)
    rank_all = bucket_rank(owner_all, groups)
    block_ids = jnp.arange(groups * depth, dtype=jnp.int32)
    source_x = block_ids // depth
    source_z = block_ids % depth
    target = source_z[:, None] * (groups * capacity) + source_x[:, None] * capacity + rank_all
    target = jnp.where(owner_all == lax.axis_index("gx"), target, -1).reshape(-1)
    select = (target[:, None] == jnp.arange(tile, dtype=jnp.int32)[None, :]).astype(jnp.bfloat16)
    tile_rows = jnp.einsum(
        "ks,kw->sw", select, every_rows, preferred_element_type=jnp.float32
    ).astype(jnp.bfloat16)
    projected = project(tile_rows, steering, steps)
    shared = lax.psum_scatter(projected, ("gx", "gy"), scatter_dimension=1, tiled=True)
    table = spectral_rows(FREQS, FREQS, steps)
    spectra = jnp.einsum("sft,td->sfd", table, shared, precision=lax.Precision.HIGHEST)
    far_field = lax.all_to_all(spectra, ("gx", "gy"), split_axis=1, concat_axis=2, tiled=True)
    return (e_next, h_next, poles_next, far_field)


def solution(mesh):
    return jax.shard_map(
        per_device,
        mesh=mesh,
        in_specs=(
            P(None, "gx", "gy", "gz"),
            P(None, "gx", "gy", "gz"),
            P("gx", "gy", "gz"),
            P("gx", "gy", "gz"),
            P(None, None, "gx", "gy", "gz"),
            P(),
            P(),
            P(("gx", "gy", "gz")),
            P(("gx", "gy", "gz"), None),
            P(None, None, ("gx", "gy", "gz")),
            P(None, ("gx", "gy"), "gz"),
        ),
        out_specs=(
            P(None, "gx", "gy", "gz"),
            P(None, "gx", "gy", "gz"),
            P(None, None, "gx", "gy", "gz"),
            P(None, ("gx", "gy"), "gz"),
        ),
        check_vma=False,
    )
```

profile of v0, /device:TPU:1, one launch (start us, length us, event | category | flops | bytes accessed | tf_op | source)
XLA Modules:
  0.0 739.0 jit_solution(13356174552181761988)
XLA Ops:
  7.2 1.1 constant_dynamic-update-slice_fusion.1
  9.3 5.1 collective-permute-start.1
  14.4 1.9 collective-permute-start
  16.4 1.3 dynamic-slice
  19.1 13.5 %all-reduce = s32[1024]{0:T(1024)S(1)} all-reduce(s32[1024]{0:T(1024)S(1)} %bitcast_dynamic-update-slice_fusion), channel_id=1, replica_groups=mesh['gx'=16,'gy'=8,'gz'=2] {'gx','gz'}, use_global_device_ids=true, to_apply=%add | all-reduce | flops 1024 | bytes 8192
  32.7 1.5 broadcast_divide_fusion
  34.2 1.5 broadcast_compare_fusion
  35.7 1.0 fusion.36
  38.4 1.3 collective-permute-start.3
  39.7 4.2 collective-permute-start.2
  45.0 1.1 fusion.34
  46.1 1.6 copy.112
  47.6 1.3 collective-permute-start.5
  49.4 6.1 collective-permute-start.4
  56.6 2.1 copy.95
  58.6 2.0 pad_maximum_fusion
  62.5 1.4 fusion.33
  64.1 3.3 copy.99
  67.4 3.4 gather_fusion
  71.4 70.4 %all_gather.7 = bf16[1024,256]{1,0:T(8,128)(2,1)S(1)} all-gather(bf16[32,256]{1,0:T(8,128)(2,1)S(1)} %copy.103), channel_id=1, replica_groups=mesh['gx'=16,'gy'=8,'gz'=2] {'gx','gz'}, dimensions={0}, use_global_device_ids=true | all-gather | bytes 540672 | tf_op jit(solution)/shard_map/all_gather | solution.py:120
  142.4 1.9 convolution_bitcast_fusion
  144.6 553.2 %reduce-scatter.2.cloned.1.call-done = f32[64,16]{0,1:T(8,128)} async-done(((f32[64,2048]{0,1:T(8,128)}), f32[64,16]{0,1:T(8,128)}) %reduce-scatter.2.cloned.1.call-update) | async-done | bytes 4112 | tf_op jit(solution)/shard_map/reduce_scatter | solution.py:135
  699.5 18.1 %all-to-all-start = ((f32[2,256,16]{2,0,1:T(2,128)}), f32[2,256,16]{2,0,1:T(2,128)S(1)}, u32[]{:S(2)}, u32[]{:S(2)}) async-start(f32[2,256,16]{2,0,1:T(2,128)} %copy.107), calls=%async_computation.1 | async-start | bytes 524288 | tf_op jit(solution)/shard_map/all_to_all | solution.py:138
  718.4 12.9 %all-to-all-done = f32[2,256,16]{2,0,1:T(2,128)S(1)} async-done(((f32[2,256,16]{2,0,1:T(2,128)}), f32[2,256,16]{2,0,1:T(2,128)S(1)}, u32[]{:S(2)}, u32[]{:S(2)}) %all-to-all-start) | async-done | bytes 32800 | tf_op jit(solution)/shard_map/all_to_all | solution.py:138
  (82 shorter events, 12.8 us)
Async XLA Ops:
  7.2 135.2 %copy-start = (bf16[4,128,2048]{2,1,0:T(8,128)(2,1)S(1)}, bf16[4,128,2048]{2,1,0:T(8,128)(2,1)}, u32[]{:S(2)}) copy-start(bf16[4,128,2048]{2,1,0:T(8,128)(2,1)} %param.21) | copy-start | bytes 6291460
  7.2 36.7 %copy-start.11 = (s32[32]{0:T(128)S(1)}, s32[32]{0:T(128)}, u32[]{:S(2)}) copy-start(s32[32]{0:T(128)} %param.18) | copy-start | bytes 388
  7.2 690.6 %reduce-scatter.2.cloned.1.call-start = ((), (), s32[]{:S(2)}) async-start(), calls=%async_computation.2 | async-start | bytes 1056768 | tf_op jit(solution)/shard_map/reduce_scatter | solution.py:135
  9.3 29.1 %collective-permute-start.1 = (f32[6,1,16,128]{3,2,1,0:T(8,128)S(1)}, f32[6,1,16,128]{3,2,1,0:T(8,128)S(1)}, u32[]{:S(2)}, u32[]{:S(2)}) collective-permute-start(f32[6,1,16,128]{3,2,1,0:T(8,128)S(1)} %get-tuple-element.28), channel_id=1, source_target_pairs={{16,0},{32,16},{48,32},{64,48},{80,64},{96,80},{112,96},{128,112},... | collective-permute-start | bytes 147464 | tf_op jit(solution)/shard_map/ppermute | solution.py:19
  14.4 23.9 %collective-permute-start = (f32[6,1,16,128]{3,2,1,0:T(8,128)S(1)}, f32[6,1,16,128]{3,2,1,0:T(8,128)S(1)}, u32[]{:S(2)}, u32[]{:S(2)}) collective-permute-start(f32[6,1,16,128]{3,2,1,0:T(8,128)S(1)} %get-tuple-element.27), channel_id=1, source_target_pairs={{0,16},{16,32},{32,48},{48,64},{64,80},{80,96},{96,112},{112,128},... | collective-permute-start | bytes 147464 | tf_op jit(solution)/shard_map/ppermute | solution.py:16
  38.4 6.0 collective-permute-start.3
  39.7 5.2 collective-permute-start.2
  47.6 8.4 %collective-permute-start.5 = (f32[6,10,18,1]{2,3,1,0:T(1,128)S(1)}, f32[6,10,18,1]{2,3,1,0:T(1,128)S(1)}, u32[]{:S(2)}, u32[]{:S(2)}) collective-permute-start(f32[6,10,18,1]{2,3,1,0:T(1,128)S(1)} %copy.112), channel_id=1, source_target_pairs={{1,0},{3,2},{5,4},{7,6},{9,8},{11,10},{13,12},{15,14},{17,16},{19,... | collective-permute-start | bytes 12968 | tf_op jit(solution)/shard_map/ppermute | solution.py:19
  49.4 7.2 collective-permute-start.4
  61.1 1.4 copy-start.1
  61.1 1.4 copy-start.8
  61.1 1.4 copy-start.9
  62.5 1.5 copy-start.2
  62.5 1.5 copy-start.4
  62.5 1.5 copy-start.5
  64.0 3.4 copy-start.3
  64.1 6.9 copy-start.10
  64.1 7.0 copy-start.6
  64.1 77.7 %copy-start.7 = (s32[1024,1]{0,1:T(1,128)S(1)}, s32[1024,1]{0,1:T(1,128)}, u32[]{:S(2)}) copy-start(s32[1024,1]{0,1:T(1,128)} %reshape_select_fusion) | copy-start | bytes 12292
  699.5 31.8 %all-to-all-start = ((f32[2,256,16]{2,0,1:T(2,128)}), f32[2,256,16]{2,0,1:T(2,128)S(1)}, u32[]{:S(2)}, u32[]{:S(2)}) async-start(f32[2,256,16]{2,0,1:T(2,128)} %copy.107), calls=%async_computation.1 | async-start | bytes 524288 | tf_op jit(solution)/shard_map/all_to_all | solution.py:138
Sparse Core Ops, SparseCore 0:
  144.4 553.2 reduce-scatter.1
where the time goes:
time: 740 us; the launch traced here: 739 us
  waiting for transfers between devices  567 us (77%)
  blocking collectives  83.9 us (11%)
  starting transfers between devices  38 us (5%)
  local copies, waits for them, and re-layouts  21 us (3%)
  between operations  15.1 us (2%)
  other arithmetic  11.1 us (2%)
    reduce_scatter x1, waiting for transfers between devices, per_device(): lax.psum_scatter(projected, ('gx', 'gy'), scatter_dimension=1, tiled=True)  553 us
    all_gather x1, blocking collectives, per_device(): lax.all_gather(sample_rows, ('gx', 'gz'), axis=0, tiled=True)  70.4 us
    all_to_all x1, starting transfers between devices, per_device(): lax.all_to_all(spectra, ('gx', 'gy'), split_axis=1, concat_axis=2, tiled=...  18.1 us
  transfers between devices with their start and end apart: 8, of which 3 were waited for; matrix products, arithmetic and copies ran while one was open for 1% of the time, Pallas kernels for 0%

commit v1 on v0

v1 whole, which is shorter than its diff:
```python
import math

import jax
import jax.numpy as jnp
import numpy as np
from jax import lax
from jax.experimental import pallas as pl
from jax.experimental.pallas import tpu as pltpu
from jax.sharding import PartitionSpec as P

FREQS = 256
F32 = jnp.float32
BF16 = jnp.bfloat16
VM = pl.BlockSpec(memory_space=pltpu.VMEM)
SM = pl.BlockSpec(memory_space=pltpu.SMEM)


def call(body, out_shape, in_specs, scratch=(), flops=0, data=0):
    many = isinstance(out_shape, (list, tuple))
    return pl.pallas_call(
        body,
        out_shape=out_shape,
        in_specs=in_specs,
        out_specs=[VM] * len(out_shape) if many else VM,
        scratch_shapes=list(scratch),
        compiler_params=pltpu.CompilerParams(vmem_limit_bytes=32 << 20),
        cost_estimate=pl.CostEstimate(flops=flops, bytes_accessed=data, transcendentals=0),
    )


def struct(*shape, dtype=F32):
    return jax.ShapeDtypeStruct(shape, dtype)


def lanes(*shape):
    return lax.broadcasted_iota(jnp.int32, shape, len(shape) - 1)


def rows(*shape):
    return lax.broadcasted_iota(jnp.int32, shape, len(shape) - 2)


def dot_t(a, b):
    return lax.dot_general(a, b, (((0,), (0,)), ((), ())), preferred_element_type=F32)


def face_body(e_ref, fx_ref, fy_ref, fz_ref):
    nx = e_ref.shape[1]
    fx_ref[0] = e_ref[1, 0]
    fx_ref[1] = e_ref[2, 0]
    lane = lanes(16, 128)
    for part, comp in enumerate((0, 2)):
        for i in range(nx):
            fy_ref[part, i : i + 1, :] = e_ref[comp, i, 0:1, :]
    for part, comp in enumerate((0, 1)):
        acc = jnp.zeros((16, 128), F32)
        for i in range(nx):
            moved = e_ref[comp, i] if i == 0 else pltpu.roll(e_ref[comp, i], i, 1)
            acc = jnp.where(lane == i, moved, acc)
        fz_ref[part] = acc


def mag_body(keep, e_ref, h_ref, hx_ref, hy_ref, hz_ref, out_ref, gx_ref, gy_ref, gz_ref):
    nx = e_ref.shape[1]
    lane = lanes(16, 128)
    row = rows(16, 128)
    up_x = [hx_ref[part] * keep[0] for part in range(2)]
    up_y = [hy_ref[part] * keep[1] for part in range(2)]
    up_z = [hz_ref[part] * keep[2] for part in range(2)]
    face_z = [jnp.zeros((16, 128), F32), jnp.zeros((16, 128), F32)]
    for i in range(nx):
        ex, ey, ez = e_ref[0, i], e_ref[1, i], e_ref[2, i]
        ey_x = e_ref[1, i + 1] if i + 1 < nx else up_x[0]
        ez_x = e_ref[2, i + 1] if i + 1 < nx else up_x[1]
        ex_y = jnp.where(row == 15, up_y[0][i : i + 1], pltpu.roll(ex, 15, 0))
        ez_y = jnp.where(row == 15, up_y[1][i : i + 1], pltpu.roll(ez, 15, 0))
        ex_z = jnp.where(lane == 127, pltpu.roll(up_z[0], 127 - i, 1), pltpu.roll(ex, 127, 1))
        ey_z = jnp.where(lane == 127, pltpu.roll(up_z[1], 127 - i, 1), pltpu.roll(ey, 127, 1))
        hx = h_ref[0, i] - 0.5 * ((ez_y - ez) - (ey_z - ey))
        hy = h_ref[1, i] - 0.5 * ((ex_z - ex) - (ez_x - ez))
        hz = h_ref[2, i] - 0.5 * ((ey_x - ey) - (ex_y - ex))
        out_ref[0, i] = hx
        out_ref[1, i] = hy
        out_ref[2, i] = hz
        if i == nx - 1:
            gx_ref[0] = hy
            gx_ref[1] = hz
        gy_ref[0, i : i + 1, :] = hx[15:16]
        gy_ref[1, i : i + 1, :] = hz[15:16]
        for part, value in enumerate((hx, hy)):
            face_z[part] = jnp.where(lane == i, pltpu.roll(value, (i + 1) % 128, 1), face_z[part])
    gz_ref[0] = face_z[0]
    gz_ref[1] = face_z[1]


def decay_body(decay, poles_ref, out_ref):
    for comp in range(3):
        for i in range(poles_ref.shape[2]):
            acc = decay[0] * poles_ref[0, comp, i]
            for p in range(1, poles_ref.shape[0]):
                acc = acc + decay[p] * poles_ref[p, comp, i]
            out_ref[comp, i] = acc


def elec_body(
    keep, gain, e_ref, h_ref, hx_ref, hy_ref, hz_ref, eps_ref, wall_ref, kept_ref, prep_ref,
    e_out, drive_out, pack_out, cells,
):
    nx = e_ref.shape[1]
    lane = lanes(16, 128)
    row = rows(16, 128)
    dn_x = [hx_ref[part] * keep[3] for part in range(2)]
    dn_y = [hy_ref[part] * keep[4] for part in range(2)]
    dn_z = [hz_ref[part] * keep[5] for part in range(2)]
    total = gain[0]
    for p in range(1, gain.shape[0]):
        total = total + gain[p]
    for i in range(nx):
        hx, hy, hz = h_ref[0, i], h_ref[1, i], h_ref[2, i]
        hy_x = h_ref[1, i - 1] if i else dn_x[0]
        hz_x = h_ref[2, i - 1] if i else dn_x[1]
        hx_y = jnp.where(row == 0, dn_y[0][i : i + 1], pltpu.roll(hx, 1, 0))
        hz_y = jnp.where(row == 0, dn_y[1][i : i + 1], pltpu.roll(hz, 1, 0))
        low = [v if i == 0 else pltpu.roll(v, 128 - i, 1) for v in dn_z]
        hx_z = jnp.where(lane == 0, low[0], pltpu.roll(hx, 1, 1))
        hy_z = jnp.where(lane == 0, low[1], pltpu.roll(hy, 1, 1))
        drive = [
            (hz - hz_y) - (hy - hy_z),
            (hx - hx_z) - (hz - hz_x),
            (hy - hy_x) - (hx - hx_y),
        ]
        half = 0.5 / eps_ref[i]
        wall = wall_ref[i] == 1
        for comp in range(3):
            field = jnp.where(
                wall, kept_ref[comp, i] + total * drive[comp], e_ref[comp, i] + half * drive[comp]
            )
            e_out[comp, i] = field
            drive_out[comp, i] = drive[comp]
            if comp < 2:
                cells[comp, i * 16 : (i + 1) * 16, :] = field.astype(BF16)
        cells[2, i * 16 : (i + 1) * 16, :] = hx.astype(BF16)
        cells[3, i * 16 : (i + 1) * 16, :] = hy.astype(BF16)
    pick = prep_ref[2].astype(BF16)
    at = prep_ref[3]
    lane = lanes(32, 128)
    packed = jnp.zeros((128, 128), F32)
    for half in range(2):
        wide = jnp.zeros((32, 128), F32)
        for e in range(2):
            found = jnp.dot(pick, cells[2 * half + e], preferred_element_type=F32)
            value = jnp.sum(found * at, axis=1, keepdims=True)
            wide = jnp.where(lane == 64 * e + 63, value, wide)
        packed = packed + dot_t(prep_ref[half].astype(BF16), wide.astype(BF16))
    pack_out[0] = packed
    pack_out[1] = packed


def poles_body(decay, gain, poles_ref, drive_ref, out_ref):
    for comp in range(3):
        for i in range(poles_ref.shape[2]):
            drive = drive_ref[comp, i]
            for p in range(poles_ref.shape[0]):
                out_ref[p, comp, i] = decay[p] * poles_ref[p, comp, i] + gain[p] * drive


def pack_body(owner_ref, cell_ref, hist_ref, prep_out, pack_out):
    lane = lanes(32, 128)
    owner = owner_ref[...]
    onehot = jnp.where(lane == owner, 1.0, 0.0)
    earlier = jnp.where(lanes(32, 32) < rows(32, 32), 1.0, 0.0).astype(BF16)
    count = jnp.dot(earlier, onehot.astype(BF16), preferred_element_type=F32)
    rank = jnp.sum(count * onehot, axis=1, keepdims=True).astype(jnp.int32)
    slot = owner * 8 + rank
    cell = cell_ref[...]
    prep_out[2] = jnp.where(lane == (cell >> 7), 1.0, 0.0)
    prep_out[3] = jnp.where(lane == (cell & 127), 1.0, 0.0)
    packed = jnp.zeros((128, 128), F32)
    for half in range(2):
        select = jnp.where(lane == slot + 4 * half, 1.0, 0.0)
        prep_out[half] = select
        packed = packed + lax.dot_general(
            select.T.astype(BF16),
            hist_ref[half * 128 : (half + 1) * 128, :],
            (((1,), (1,)), ((), ())),
            preferred_element_type=F32,
        )
    pack_out[0] = packed
    pack_out[1] = packed


def tile_rows(got_ref, first):
    got = got_ref[...].astype(BF16)
    row, slot = rows(256, 128), lanes(256, 128)
    parts = []
    for half in range(2):
        place = jnp.where(row == (slot >> 2) * 8 + 4 * half + (slot & 3), 1.0, 0.0).astype(BF16)
        moved = dot_t(got, place).astype(BF16)
        parts += [moved[first:64], moved[64 + first : 128]]
    return jnp.concatenate(parts, axis=1)


def project_body(got_ref, steer_ref, out_ref):
    series = tile_rows(got_ref, 0)
    for n in range(8):
        part = jnp.dot(series, steer_ref[:, n * 256 : (n + 1) * 256], preferred_element_type=F32)
        out_ref[2 * n] = part[:, :128]
        out_ref[2 * n + 1] = part[:, 128:]


def spectrum_body(got_ref, steer_ref, sums_ref, table_ref, out_ref, last):
    series = tile_rows(got_ref, 48)
    for n in range(8):
        part = jnp.dot(series, steer_ref[:, n * 256 : (n + 1) * 256], preferred_element_type=F32)
        last[2 * n : 2 * n + 1, :] = part[15:16, :128]
        last[2 * n + 1 : 2 * n + 2, :] = part[15:16, 128:]
    projected = sums_ref[0]
    for a in range(1, sums_ref.shape[0]):
        projected = projected + sums_ref[a]
    for b in range(8):
        out_ref[b, 0:64, :] = jnp.dot(
            table_ref[b], projected, precision=lax.Precision.HIGHEST, preferred_element_type=F32
        )
        out_ref[b, 64:80, :] = last[...]


def regroup_body(got_ref, out_ref):
    total = got_ref[0]
    for b in range(1, got_ref.shape[0]):
        total = total + got_ref[b]
    for a in range(16):
        out_ref[a, 0:4, :] = total[4 * a : 4 * a + 4]
        out_ref[a, 8:24, :] = total[64:80]


def finish_body(weight, got_ref, out_ref):
    last = got_ref[0, 8:24, :]
    for a in range(1, 16):
        last = last + got_ref[a, 8:24, :]
    for a in range(16):
        for s in range(2):
            for f in range(2):
                out_ref[s, f : f + 1, a * 128 : (a + 1) * 128] = (
                    got_ref[a, 2 * s + f : 2 * s + f + 1, :] + weight[s, f] * last[a : a + 1]
                )


def spectral_table(steps):
    times = np.arange(steps, dtype=np.float64)
    levels = np.arange(FREQS, dtype=np.float64) + 0.5
    phase = math.pi / (2.0 * FREQS) * levels[:, None] * times[None, :]
    table = np.stack([np.cos(phase), -np.sin(phase)]) / math.sqrt(steps)
    return table.astype(np.float32)


def shift(value, axis, step):
    count = lax.axis_size(axis)
    return lax.ppermute(value, axis, [(i, (i + step) % count) for i in range(count)])


def per_device(
    e_field, h_field, permittivity, wall_mask, poles, pole_decay, pole_gain, face_cells, owners,
    history, steering,
):
    nx, ny, nz = e_field.shape[1:]
    steps = history.shape[0] + 1
    axes = ("gx", "gy", "gz")
    places = [lax.axis_index(axis) for axis in axes]
    keep = jnp.stack(
        [(at < lax.axis_size(axis) - 1) for at, axis in zip(places, axes)]
        + [at > 0 for at in places]
    ).astype(F32)
    block = struct(3, nx, ny, nz)
    faces = [struct(2, ny, nz), struct(2, nx, nz), struct(2, ny, 128)]

    near = call(face_body, faces, [VM], data=200000)(e_field)
    up = [shift(face, axis, -1) for face, axis in zip(near, axes)]

    past = jnp.transpose(history, (1, 0, 2))
    past = jnp.pad(past, ((0, 0), (0, 1), (0, 0))).reshape(4 * steps, -1)
    prep, leaving = call(pack_body, [struct(4, 32, 128), struct(2, 128, 128)], [VM] * 3, data=200000)(
        owners, face_cells.reshape(-1, 1), past
    )

    def to_tiles(packed):
        moved = lax.all_to_all(packed.reshape(32, 8, 128), ("gz", "gx"), 0, 0, tiled=True)
        return moved.reshape(256, 128)

    arrived = to_tiles(leaving)

    h_next, *far = call(mag_body, [block, *faces], [SM] + [VM] * 5, data=600000)(
        keep, e_field, h_field, *up
    )
    down = [shift(face, axis, 1) for face, axis in zip(far, axes)]
    kept = call(decay_body, block, [SM, VM], data=1800000)(pole_decay, poles)

    weights = steering.reshape(-1, steering.shape[2])
    part = call(project_body, struct(16, 64, 128), [VM] * 2, flops=1 << 27, data=2600000)(
        arrived, weights
    )
    sums = lax.all_to_all(part, "gx", 0, 0, tiled=True)

    e_next, drive, fresh = call(
        elec_body,
        [block, block, struct(2, 128, 128)],
        [SM] * 2 + [VM] * 9,
        scratch=[pltpu.VMEM((4, 128, 128), BF16)],
        data=1200000,
    )(keep, pole_gain, e_field, h_next, *down, permittivity, wall_mask, kept, prep)
    latest = to_tiles(fresh)
    poles_next = call(poles_body, struct(*poles.shape), [SM] * 2 + [VM] * 2, data=3400000)(
        pole_decay, pole_gain, poles, drive
    )

    table = spectral_table(steps)
    ordered = table.reshape(2, 16, 8, 2, steps).transpose(2, 1, 0, 3, 4).reshape(8, 64, steps)
    spectra = call(
        spectrum_body,
        struct(8, 80, 128),
        [VM] * 4,
        scratch=[pltpu.VMEM((16, 128), F32)],
        flops=1 << 27,
        data=2600000,
    )(latest, weights, sums, jnp.asarray(ordered))
    spectra = lax.all_to_all(spectra, "gy", 0, 0, tiled=True)
    blocks = call(regroup_body, struct(16, 24, 128), [VM], data=500000)(spectra)
    blocks = lax.all_to_all(blocks, "gx", 0, 0, tiled=True)
    mine = places[0] * 8 + places[1]
    weight = lax.dynamic_slice(jnp.asarray(table[:, :, -1]), (0, 2 * mine), (2, 2))
    far_field = call(finish_body, struct(2, 2, 2048), [SM, VM], data=200000)(weight, blocks)
    return (e_next, h_next, poles_next, far_field)


def solution(mesh):
    return jax.shard_map(
        per_device,
        mesh=mesh,
        in_specs=(
            P(None, "gx", "gy", "gz"),
            P(None, "gx", "gy", "gz"),
            P("gx", "gy", "gz"),
            P("gx", "gy", "gz"),
            P(None, None, "gx", "gy", "gz"),
            P(),
            P(),
            P(("gx", "gy", "gz")),
            P(("gx", "gy", "gz"), None),
            P(None, None, ("gx", "gy", "gz")),
            P(None, ("gx", "gy"), "gz"),
        ),
        out_specs=(
            P(None, "gx", "gy", "gz"),
            P(None, "gx", "gy", "gz"),
            P(None, None, "gx", "gy", "gz"),
            P(None, ("gx", "gy"), "gz"),
        ),
        check_vma=False,
    )
```

time: 740 us -> 98 us (0.13)
  waiting for transfers between devices: 567 us -> 14 us
  blocking collectives: 83.9 us -> 28 us
  between operations: 15.1 us -> 0.81 us
  local copies, waits for them, and re-layouts: 21 us -> 8.43 us
  other arithmetic: 11.1 us -> 0.01 us
  Pallas kernels: 0 us -> 10.3 us
    reduce_scatter x1 -> x0, waiting for transfers between devices: 553 us -> none  [per_device(): lax.psum_scatter(projected, ('gx', 'gy'), scatter_dimension=1, tiled=True)]
    all_gather x1 -> x0, blocking collectives: 70.4 us -> none  [per_device(): lax.all_gather(sample_rows, ('gx', 'gz'), axis=0, tiled=True)]
    all_to_all x0 -> x2, blocking collectives: none -> 28 us  [the longest x1 15.2 us: per_device(): spectra = lax.all_to_all(spectra, 'gy', 0, 0, tiled=True)]
    unnamed x1 -> x0, blocking collectives: 13.5 us -> none
    pallas_call x0 -> x10, Pallas kernels: none -> 10.3 us  [the longest x1 1.86 us: per_device(): call(poles_body, struct(*poles.shape), [SM] * 2 + [VM] * 2, data=3400000)]
    ppermute x6, starting transfers between devices: 19.9 us -> 11.5 us  [shift(): lax.ppermute(value, axis, [(i, (i + step) % count) for i in range(count)])]
    all_to_all x1 -> x3, starting transfers between devices: 18.1 us -> 24.4 us  [the longest x2 17.9 us: to_tiles(): lax.all_to_all(packed.reshape(32, 8, 128), ('gz', 'gx'), 0, 0, tiled=True)]
  transfers between devices with their start and end apart: 8 -> 9, of which waited for: 3 -> 4; matrix products, arithmetic and copies ran while one was open for 1% -> 0% of each run, Pallas kernels for 0% -> 7%
where the time goes in v1:
time: 98 us; the launch traced here: 97.3 us
  starting transfers between devices  35.9 us (37%)
  blocking collectives  28 us (29%)
  waiting for transfers between devices  14 us (14%)
  Pallas kernels  10.3 us (11%)
  local copies, waits for them, and re-layouts  8.43 us (9%)
    all_to_all x2, starting transfers between devices, to_tiles(): lax.all_to_all(packed.reshape(32, 8, 128), ('gz', 'gx'), 0, 0, tiled=True)  17.9 us
    all_to_all x1, blocking collectives, per_device(): spectra = lax.all_to_all(spectra, 'gy', 0, 0, tiled=True)  15.2 us
    all_to_all x1, blocking collectives, per_device(): sums = lax.all_to_all(part, 'gx', 0, 0, tiled=True)  12.8 us
    ppermute x6, starting transfers between devices, shift(): lax.ppermute(value, axis, [(i, (i + step) % count) for i in range(count)])  11.5 us
    unnamed x32, local copies, waits for them, and re-layouts  7.43 us
    all_to_all x2, waiting for transfers between devices, to_tiles(): lax.all_to_all(packed.reshape(32, 8, 128), ('gz', 'gx'), 0, 0, tiled=True)  6.96 us
    all_to_all x1, starting transfers between devices, per_device(): blocks = lax.all_to_all(blocks, 'gx', 0, 0, tiled=True)  6.46 us
    all_to_all x1, waiting for transfers between devices, per_device(): blocks = lax.all_to_all(blocks, 'gx', 0, 0, tiled=True)  4.78 us
  transfers between devices with their start and end apart: 9, of which 4 were waited for; matrix products, arithmetic and copies ran while one was open for 0% of the time, Pallas kernels for 7%

profile of v1, /device:TPU:1, one launch (start us, length us, event | category | flops | bytes accessed | tf_op | source)
XLA Modules:
  0.0 97.3 jit_solution(14914386729898505513)
XLA Ops:
  0.7 0.8 copy.19.cell_ref
  2.2 0.9 copy.20
  3.1 1.2 %shard_map.159 = (f32[4,32,128]{2,1,0:T(8,128)S(1)}, f32[2,128,128]{2,1,0:T(8,128)}) custom-call(s32[32,1]{1,0:T(8,128)S(1)} %copy.18.owner_ref, s32[32,1]{1,0:T(8,128)S(1)} %copy.19.cell_ref, bf16[256,32]{1,0:T(8,128)(2,1)S(1)} %bitcast.18), custom_call_target="tpu_custom_call" | custom-call | bytes 200000 | tf_op jit(solution)/shard_map/pallas_call | solution.py:281
  4.3 8.6 %all-to-all-start.1 = ((f32[32,8,128]{2,1,0:T(8,128)}), f32[32,8,128]{2,1,0:T(8,128)S(1)}, u32[]{:S(2)}, u32[]{:S(2)}) async-start(f32[32,8,128]{2,1,0:T(8,128)} %bitcast.12), calls=%async_computation.1 | async-start | bytes 262144 | tf_op jit(solution)/shard_map/all_to_all | solution.py:286
  13.0 0.9 copy-done.3
  14.3 3.0 %collective-permute-start.2 = (f32[2,16,128]{2,1,0:T(8,128)S(1)}, f32[2,16,128]{2,1,0:T(8,128)S(1)}, u32[]{:S(2)}, u32[]{:S(2)}) collective-permute-start(f32[2,16,128]{2,1,0:T(8,128)S(1)} %get-tuple-element.18), channel_id=1, source_target_pairs={{0,1},{1,0},{2,3},{3,2},{4,5},{5,4},{6,7},{7,6},{8,9},{9,8},{10,11... | collective-permute-start | bytes 49160 | tf_op jit(solution)/shard_map/ppermute | solution.py:258
  17.3 5.6 %collective-permute-start.1 = (f32[2,8,128]{2,1,0:T(8,128)S(1)}, f32[2,8,128]{2,1,0:T(8,128)S(1)}, u32[]{:S(2)}, u32[]{:S(2)}) collective-permute-start(f32[2,8,128]{2,1,0:T(8,128)S(1)} %get-tuple-element.17), channel_id=1, source_target_pairs={{0,14},{2,0},{4,2},{6,4},{8,6},{10,8},{12,10},{14,12},{1,15},{3,1}... | collective-permute-start | bytes 24584 | tf_op jit(solution)/shard_map/ppermute | solution.py:258
  23.7 0.9 copy-done.4
  24.6 0.9 copy-done.7
  25.5 1.4 %shard_map.157 = (f32[3,8,16,128]{3,2,1,0:T(8,128)}, f32[2,16,128]{2,1,0:T(8,128)S(1)}, f32[2,8,128]{2,1,0:T(8,128)S(1)}, f32[2,16,128]{2,1,0:T(8,128)S(1)}) custom-call(f32[6]{0:T(128)S(1)} %convert_element_type.5.keep, f32[3,8,16,128]{3,2,1,0:T(8,128)S(1)} %copy-done.4, f32[3,8,16,128]{3,2,1,0:T(8,128)S(1)} %copy-done.7, ...), custom_call_target="tpu_custom_call" | custom-call | bytes 600000 | tf_op jit(solution)/shard_map/pallas_call | solution.py:291
  26.9 2.5 %collective-permute-start.3 = (f32[2,16,128]{2,1,0:T(8,128)S(1)}, f32[2,16,128]{2,1,0:T(8,128)S(1)}, u32[]{:S(2)}, u32[]{:S(2)}) collective-permute-start(f32[2,16,128]{2,1,0:T(8,128)S(1)} %get-tuple-element.20), channel_id=1, source_target_pairs={{0,16},{16,32},{32,48},{48,64},{64,80},{80,96},{96,112},{112,128},... | collective-permute-start | bytes 49160 | tf_op jit(solution)/shard_map/ppermute | solution.py:258
  29.5 1.4 %copy-done.1 = f32[8,3,8,16,128]{4,3,2,1,0:T(8,128)S(1)} copy-done((f32[8,3,8,16,128]{4,3,2,1,0:T(8,128)S(1)}, f32[8,3,8,16,128]{4,3,2,1,0:T(8,128)}, u32[]{:S(2)}) %copy-start.1) | copy-done | bytes 1572888
  32.2 1.6 %collective-permute-done.4.hy_ref = f32[2,8,128]{2,1,0:T(8,128)S(1)} collective-permute-done((f32[2,8,128]{2,1,0:T(8,128)S(1)}, f32[2,8,128]{2,1,0:T(8,128)S(1)}, u32[]{:S(2)}, u32[]{:S(2)}) %collective-permute-start.4) | collective-permute-done | bytes 8224 | tf_op jit(solution)/shard_map/ppermute | solution.py:258
  33.8 0.9 copy-done.8
  34.7 1.7 %shard_map.160 = (f32[3,8,16,128]{3,2,1,0:T(8,128)}, f32[3,8,16,128]{3,2,1,0:T(8,128)S(1)}, f32[2,128,128]{2,1,0:T(8,128)}) custom-call(f32[6]{0:T(128)S(1)} %convert_element_type.5.keep, f32[8]{0:T(128)S(1)} %copy-done.11, f32[3,8,16,128]{3,2,1,0:T(8,128)S(1)} %copy-done.5, f32[3,8,16,128]{3,2,1,0:T(8,128)S(1)} %copy-done.8, ...), custom_call_target="tpu_custom_call" | custom-call | bytes 1200000 | tf_op jit(solution)/shard_map/pallas_call | solution.py:303
  36.5 9.3 %all-to-all-start = ((f32[32,8,128]{2,1,0:T(8,128)}), f32[32,8,128]{2,1,0:T(8,128)S(1)}, u32[]{:S(2)}, u32[]{:S(2)}) async-start(f32[32,8,128]{2,1,0:T(8,128)} %bitcast.9), calls=%async_computation | async-start | bytes 262144 | tf_op jit(solution)/shard_map/all_to_all | solution.py:286
  46.5 7.0 %all-to-all-done = f32[32,8,128]{2,1,0:T(8,128)S(1)} async-done(((f32[32,8,128]{2,1,0:T(8,128)}), f32[32,8,128]{2,1,0:T(8,128)S(1)}, u32[]{:S(2)}, u32[]{:S(2)}) %all-to-all-start) | async-done | bytes 131104 | tf_op jit(solution)/shard_map/all_to_all | solution.py:286
  53.4 12.8 %all_to_all.25.sums_ref = f32[16,64,128]{2,1,0:T(8,128)S(1)} all-to-all(f32[16,64,128]{2,1,0:T(8,128)S(1)} %shard_map.162), channel_id=1, replica_groups=mesh['gx'=16,'gy'=8,'gz'=2] {'gx'}, dimensions={0} | all-to-all | bytes 1048576 | tf_op jit(solution)/shard_map/all_to_all | solution.py:301
  66.2 0.8 shard_map.163
  67.1 15.2 %all_to_all.26.got_ref = f32[8,80,128]{2,1,0:T(8,128)S(1)} all-to-all(f32[8,80,128]{2,1,0:T(8,128)S(1)} %shard_map.163), channel_id=1, replica_groups=mesh['gx'=16,'gy'=8,'gz'=2] {'gy'}, dimensions={0} | all-to-all | bytes 655360 | tf_op jit(solution)/shard_map/all_to_all | solution.py:325
  82.9 6.5 %all-to-all-start.4 = ((f32[16,24,128]{2,1,0:T(8,128)}), f32[16,24,128]{2,1,0:T(8,128)S(1)}, u32[]{:S(2)}, u32[]{:S(2)}) async-start(f32[16,24,128]{2,1,0:T(8,128)} %shard_map.164), calls=%async_computation.4 | async-start | bytes 393216 | tf_op jit(solution)/shard_map/all_to_all | solution.py:327
  89.5 1.9 %shard_map.161 = f32[8,3,8,16,128]{4,3,2,1,0:T(8,128)} custom-call(f32[8]{0:T(128)S(1)} %copy-done.13, f32[8]{0:T(128)S(1)} %copy-done.11, f32[8,3,8,16,128]{4,3,2,1,0:T(8,128)S(1)} %copy-done.2, f32[3,8,16,128]{3,2,1,0:T(8,128)S(1)} %get-tuple-element.25.drive_ref), custom_call_target="tpu_custom_call" | custom-call | bytes 3400000 | tf_op jit(solution)/shard_map/pallas_call | solution.py:311
  91.4 4.8 %all-to-all-done.4.got_ref = f32[16,24,128]{2,1,0:T(8,128)S(1)} async-done(((f32[16,24,128]{2,1,0:T(8,128)}), f32[16,24,128]{2,1,0:T(8,128)S(1)}, u32[]{:S(2)}, u32[]{:S(2)}) %all-to-all-start.4) | async-done | bytes 196640 | tf_op jit(solution)/shard_map/all_to_all | solution.py:327
  96.1 1.2 %shard_map.165 = f32[2,2,2048]{2,1,0:T(2,128)} custom-call(f32[2,2]{1,0:T(2,128)S(1)} %constant_dynamic-slice_fusion.weight, f32[16,24,128]{2,1,0:T(8,128)S(1)} %all-to-all-done.4.got_ref), custom_call_target="tpu_custom_call" | custom-call | bytes 200000 | tf_op jit(solution)/shard_map/pallas_call | solution.py:330
  (43 shorter events, 4.8 us)
Async XLA Ops:
  0.6 33.1 %copy-start.5 = (f32[3,8,16,128]{3,2,1,0:T(8,128)S(1)}, f32[3,8,16,128]{3,2,1,0:T(8,128)}, u32[]{:S(2)}) copy-start(f32[3,8,16,128]{3,2,1,0:T(8,128)} %e_ref.5) | copy-start | bytes 589828
  0.6 33.1 %copy-start.11 = (f32[8]{0:T(128)S(1)}, f32[8]{0:T(128)}, u32[]{:S(2)}) copy-start(f32[8]{0:T(128)} %gain.3) | copy-start | bytes 100
  0.7 33.1 %copy-start.10 = (s32[8,16,128]{2,1,0:T(8,128)S(1)}, s32[8,16,128]{2,1,0:T(8,128)}, u32[]{:S(2)}) copy-start(s32[8,16,128]{2,1,0:T(8,128)} %wall_ref.1) | copy-start | bytes 196612
  0.7 33.1 %copy-start.9 = (f32[8,16,128]{2,1,0:T(8,128)S(1)}, f32[8,16,128]{2,1,0:T(8,128)}, u32[]{:S(2)}) copy-start(f32[8,16,128]{2,1,0:T(8,128)} %eps_ref.1) | copy-start | bytes 196612
  4.3 32.1 %all-to-all-start.1 = ((f32[32,8,128]{2,1,0:T(8,128)}), f32[32,8,128]{2,1,0:T(8,128)S(1)}, u32[]{:S(2)}, u32[]{:S(2)}) async-start(f32[32,8,128]{2,1,0:T(8,128)} %bitcast.12), calls=%async_computation.1 | async-start | bytes 262144 | tf_op jit(solution)/shard_map/all_to_all | solution.py:286
  12.9 0.9 copy-start.3
  14.0 9.7 %collective-permute-start = (f32[2,16,128]{2,1,0:T(8,128)S(1)}, f32[2,16,128]{2,1,0:T(8,128)S(1)}, u32[]{:S(2)}, u32[]{:S(2)}) collective-permute-start(f32[2,16,128]{2,1,0:T(8,128)S(1)} %get-tuple-element.16), channel_id=1, source_target_pairs={{0,240},{16,0},{32,16},{48,32},{64,48},{80,64},{96,80},{112,96},{1... | collective-permute-start | bytes 49160 | tf_op jit(solution)/shard_map/ppermute | solution.py:258
  14.3 9.4 %collective-permute-start.2 = (f32[2,16,128]{2,1,0:T(8,128)S(1)}, f32[2,16,128]{2,1,0:T(8,128)S(1)}, u32[]{:S(2)}, u32[]{:S(2)}) collective-permute-start(f32[2,16,128]{2,1,0:T(8,128)S(1)} %get-tuple-element.18), channel_id=1, source_target_pairs={{0,1},{1,0},{2,3},{3,2},{4,5},{5,4},{6,7},{7,6},{8,9},{9,8},{10,11... | collective-permute-start | bytes 49160 | tf_op jit(solution)/shard_map/ppermute | solution.py:258
  17.3 6.4 %collective-permute-start.1 = (f32[2,8,128]{2,1,0:T(8,128)S(1)}, f32[2,8,128]{2,1,0:T(8,128)S(1)}, u32[]{:S(2)}, u32[]{:S(2)}) collective-permute-start(f32[2,8,128]{2,1,0:T(8,128)S(1)} %get-tuple-element.17), channel_id=1, source_target_pairs={{0,14},{2,0},{4,2},{6,4},{8,6},{10,8},{12,10},{14,12},{1,15},{3,1}... | collective-permute-start | bytes 24584 | tf_op jit(solution)/shard_map/ppermute | solution.py:258
  23.0 22.8 %copy-start = (bf16[4,128,2048]{2,1,0:T(8,128)(2,1)S(1)}, bf16[4,128,2048]{2,1,0:T(8,128)(2,1)}, u32[]{:S(2)}) copy-start(bf16[4,128,2048]{2,1,0:T(8,128)(2,1)} %param.23) | copy-start | bytes 6291460
  23.7 0.9 copy-start.4
  24.6 0.9 copy-start.7
  26.9 6.9 %collective-permute-start.3 = (f32[2,16,128]{2,1,0:T(8,128)S(1)}, f32[2,16,128]{2,1,0:T(8,128)S(1)}, u32[]{:S(2)}, u32[]{:S(2)}) collective-permute-start(f32[2,16,128]{2,1,0:T(8,128)S(1)} %get-tuple-element.20), channel_id=1, source_target_pairs={{0,16},{16,32},{32,48},{48,64},{64,80},{80,96},{96,112},{112,128},... | collective-permute-start | bytes 49160 | tf_op jit(solution)/shard_map/ppermute | solution.py:258
  29.4 4.4 %collective-permute-start.5 = (f32[2,16,128]{2,1,0:T(8,128)S(1)}, f32[2,16,128]{2,1,0:T(8,128)S(1)}, u32[]{:S(2)}, u32[]{:S(2)}) collective-permute-start(f32[2,16,128]{2,1,0:T(8,128)S(1)} %get-tuple-element.22), channel_id=1, source_target_pairs={{0,1},{1,0},{2,3},{3,2},{4,5},{5,4},{6,7},{7,6},{8,9},{9,8},{10,11... | collective-permute-start | bytes 49160 | tf_op jit(solution)/shard_map/ppermute | solution.py:258
  29.5 4.3 %collective-permute-start.4 = (f32[2,8,128]{2,1,0:T(8,128)S(1)}, f32[2,8,128]{2,1,0:T(8,128)S(1)}, u32[]{:S(2)}, u32[]{:S(2)}) collective-permute-start(f32[2,8,128]{2,1,0:T(8,128)S(1)} %get-tuple-element.21), channel_id=1, source_target_pairs={{0,2},{2,4},{4,6},{6,8},{8,10},{10,12},{12,14},{14,0},{1,3},{3,5},... | collective-permute-start | bytes 24584 | tf_op jit(solution)/shard_map/ppermute | solution.py:258
  29.5 1.4 %copy-start.1 = (f32[8,3,8,16,128]{4,3,2,1,0:T(8,128)S(1)}, f32[8,3,8,16,128]{4,3,2,1,0:T(8,128)}, u32[]{:S(2)}) copy-start(f32[8,3,8,16,128]{4,3,2,1,0:T(8,128)} %poles_ref.3) | copy-start | bytes 4718596
  30.9 0.7 copy-start.12
  33.8 0.9 copy-start.8
  36.5 16.9 %all-to-all-start = ((f32[32,8,128]{2,1,0:T(8,128)}), f32[32,8,128]{2,1,0:T(8,128)S(1)}, u32[]{:S(2)}, u32[]{:S(2)}) async-start(f32[32,8,128]{2,1,0:T(8,128)} %bitcast.9), calls=%async_computation | async-start | bytes 262144 | tf_op jit(solution)/shard_map/all_to_all | solution.py:286
  45.8 20.4 %copy-start.6 = (f32[8,64,64]{2,1,0:T(8,128)S(1)}, f32[8,64,64]{2,1,0:T(8,128)}, u32[]{:S(2)}) copy-start(f32[8,64,64]{2,1,0:T(8,128)} %constant.33.clone.table_ref) | copy-start | bytes 393220
  67.0 22.4 %copy-start.14 = (f32[2,256]{1,0:T(2,128)S(1)}, f32[2,256]{1,0:T(2,128)}, u32[]{:S(2)}) copy-start(f32[2,256]{1,0:T(2,128)} %constant.34.clone) | copy-start | bytes 6148
  67.0 22.5 %copy-start.2 = (f32[8,3,8,16,128]{4,3,2,1,0:T(8,128)S(1)}, f32[8,3,8,16,128]{4,3,2,1,0:T(8,128)}, u32[]{:S(2)}) copy-start(f32[8,3,8,16,128]{4,3,2,1,0:T(8,128)} %poles_ref.3) | copy-start | bytes 4718596
  67.0 22.4 %copy-start.13 = (f32[8]{0:T(128)S(1)}, f32[8]{0:T(128)}, u32[]{:S(2)}) copy-start(f32[8]{0:T(128)} %decay.3) | copy-start | bytes 100
  82.9 13.2 %all-to-all-start.4 = ((f32[16,24,128]{2,1,0:T(8,128)}), f32[16,24,128]{2,1,0:T(8,128)S(1)}, u32[]{:S(2)}, u32[]{:S(2)}) async-start(f32[16,24,128]{2,1,0:T(8,128)} %shard_map.164), calls=%async_computation.4 | async-start | bytes 393216 | tf_op jit(solution)/shard_map/all_to_all | solution.py:327

commit v2 on v1

v2 whole, which is shorter than its diff:
```python
import math

import jax
import jax.numpy as jnp
import numpy as np
from jax import lax
from jax.experimental import pallas as pl
from jax.experimental.pallas import tpu as pltpu
from jax.sharding import PartitionSpec as P

FREQS = 256
F32 = jnp.float32
BF16 = jnp.bfloat16
VM = pl.BlockSpec(memory_space=pltpu.VMEM)
SM = pl.BlockSpec(memory_space=pltpu.SMEM)
HB = pl.BlockSpec(memory_space=pltpu.HBM)


def call(body, out_shape, in_specs, scratch=(), flops=0, data=0):
    many = isinstance(out_shape, (list, tuple))
    return pl.pallas_call(
        body,
        out_shape=out_shape,
        in_specs=in_specs,
        out_specs=[VM] * len(out_shape) if many else VM,
        scratch_shapes=list(scratch),
        compiler_params=pltpu.CompilerParams(vmem_limit_bytes=32 << 20),
        cost_estimate=pl.CostEstimate(flops=flops, bytes_accessed=data, transcendentals=0),
    )


def far_off(value):
    return pltpu.with_memory_space_constraint(value, pltpu.HBM)


def struct(*shape, dtype=F32):
    return jax.ShapeDtypeStruct(shape, dtype)


def lanes(*shape):
    return lax.broadcasted_iota(jnp.int32, shape, len(shape) - 1)


def rows(*shape):
    return lax.broadcasted_iota(jnp.int32, shape, len(shape) - 2)


def dot_t(a, b):
    return lax.dot_general(a, b, (((0,), (0,)), ((), ())), preferred_element_type=F32)


def fetch(pairs, sems):
    copies = [pltpu.make_async_copy(*pair, sems.at[n]) for n, pair in enumerate(pairs)]
    for copy in copies:
        copy.start()
    return copies


def face_body(e_far, h_far, fx_ref, fy_ref, fz_ref, e_ref, h_ref, sems):
    bring = fetch([(e_far, e_ref), (h_far, h_ref)], sems)
    bring[0].wait()
    nx = e_ref.shape[1]
    fx_ref[0] = e_ref[1, 0]
    fx_ref[1] = e_ref[2, 0]
    lane = lanes(16, 128)
    for part, comp in enumerate((0, 2)):
        for i in range(nx):
            fy_ref[part, i : i + 1, :] = e_ref[comp, i, 0:1, :]
    for part, comp in enumerate((0, 1)):
        acc = jnp.zeros((16, 128), F32)
        for i in range(nx):
            moved = e_ref[comp, i] if i == 0 else pltpu.roll(e_ref[comp, i], i, 1)
            acc = jnp.where(lane == i, moved, acc)
        fz_ref[part] = acc
    bring[1].wait()


def inner_body(e_ref, h_ref, *refs):
    count = (len(refs) - 2) // 2
    out_ref, sems = refs[count], refs[-1]
    bring = fetch(list(zip(refs[:count], refs[count + 1 : -1])), sems)
    nx = e_ref.shape[1]
    lane = lanes(16, 128)
    row = rows(16, 128)
    zero = jnp.zeros((16, 128), F32)
    for i in range(nx):
        ex, ey, ez = e_ref[0, i], e_ref[1, i], e_ref[2, i]
        ey_x = e_ref[1, i + 1] if i + 1 < nx else zero
        ez_x = e_ref[2, i + 1] if i + 1 < nx else zero
        ex_y = jnp.where(row == 15, 0.0, pltpu.roll(ex, 15, 0))
        ez_y = jnp.where(row == 15, 0.0, pltpu.roll(ez, 15, 0))
        ex_z = jnp.where(lane == 127, 0.0, pltpu.roll(ex, 127, 1))
        ey_z = jnp.where(lane == 127, 0.0, pltpu.roll(ey, 127, 1))
        out_ref[0, i] = h_ref[0, i] - 0.5 * ((ez_y - ez) - (ey_z - ey))
        out_ref[1, i] = h_ref[1, i] - 0.5 * ((ex_z - ex) - (ez_x - ez))
        out_ref[2, i] = h_ref[2, i] - 0.5 * ((ey_x - ey) - (ex_y - ex))
    for copy in bring:
        copy.wait()


def mag_body(keep, part_ref, ux_ref, uy_ref, uz_ref, out_ref, gx_ref, gy_ref, gz_ref):
    nx = part_ref.shape[1]
    lane = lanes(16, 128)
    row = rows(16, 128)
    up_x = [ux_ref[part] * (0.5 * keep[0]) for part in range(2)]
    up_y = [uy_ref[part] * (0.5 * keep[1]) for part in range(2)]
    up_z = [uz_ref[part] * (0.5 * keep[2]) for part in range(2)]
    face_z = [jnp.zeros((16, 128), F32), jnp.zeros((16, 128), F32)]
    for i in range(nx):
        ex_z, ey_z = [jnp.where(lane == 127, pltpu.roll(v, 127 - i, 1), 0.0) for v in up_z]
        ex_y, ez_y = [jnp.where(row == 15, v[i : i + 1], 0.0) for v in up_y]
        hx = part_ref[0, i] + (ey_z - ez_y)
        hy = part_ref[1, i] - ex_z
        hz = part_ref[2, i] + ex_y
        if i == nx - 1:
            hy = hy + up_x[1]
            hz = hz - up_x[0]
            gx_ref[0] = hy
            gx_ref[1] = hz
        out_ref[0, i] = hx
        out_ref[1, i] = hy
        out_ref[2, i] = hz
        gy_ref[0, i : i + 1, :] = hx[15:16]
        gy_ref[1, i : i + 1, :] = hz[15:16]
        for part, value in enumerate((hx, hy)):
            face_z[part] = jnp.where(lane == i, pltpu.roll(value, i + 1, 1), face_z[part])
    gz_ref[0] = face_z[0]
    gz_ref[1] = face_z[1]


def wall_body(decay_ref, gain_ref, poles_ref, e_ref, eps_ref, wall_ref, base_out, slope_out):
    decay = [decay_ref[0:1, p : p + 1] for p in range(poles_ref.shape[0])]
    total = jnp.sum(gain_ref[...], axis=1, keepdims=True)
    for i in range(poles_ref.shape[2]):
        wall = wall_ref[i] == 1
        slope_out[i] = jnp.where(wall, total, 0.5 / eps_ref[i])
        for comp in range(3):
            acc = decay[0] * poles_ref[0, comp, i]
            for p in range(1, poles_ref.shape[0]):
                acc = acc + decay[p] * poles_ref[p, comp, i]
            base_out[comp, i] = jnp.where(wall, acc, e_ref[comp, i])


def elec_body(
    keep, h_ref, dx_ref, dy_ref, dz_ref, base_ref, slope_ref, select_ref, cell_ref, past_ref,
    drive_out, pack_out, cells,
):
    nx = h_ref.shape[1]
    lane = lanes(16, 128)
    row = rows(16, 128)
    dn_x = [dx_ref[part] * keep[3] for part in range(2)]
    dn_y = [dy_ref[part] * keep[4] for part in range(2)]
    dn_z = [dz_ref[part] * keep[5] for part in range(2)]
    for i in range(nx):
        hx, hy, hz = h_ref[0, i], h_ref[1, i], h_ref[2, i]
        hy_x = h_ref[1, i - 1] if i else dn_x[0]
        hz_x = h_ref[2, i - 1] if i else dn_x[1]
        hx_y = jnp.where(row == 0, dn_y[0][i : i + 1], pltpu.roll(hx, 1, 0))
        hz_y = jnp.where(row == 0, dn_y[1][i : i + 1], pltpu.roll(hz, 1, 0))
        low = [v if i == 0 else pltpu.roll(v, 128 - i, 1) for v in dn_z]
        hx_z = jnp.where(lane == 0, low[0], pltpu.roll(hx, 1, 1))
        hy_z = jnp.where(lane == 0, low[1], pltpu.roll(hy, 1, 1))
        drive = [
            (hz - hz_y) - (hy - hy_z),
            (hx - hx_z) - (hz - hz_x),
            (hy - hy_x) - (hx - hx_y),
        ]
        for comp in range(3):
            drive_out[comp, i] = drive[comp]
        span = pl.ds(i * 16, 16)
        for comp in range(2):
            field = base_ref[comp, i] + slope_ref[i] * drive[comp]
            cells[comp, span, :] = field.astype(BF16)
        cells[2, span, :] = hx.astype(BF16)
        cells[3, span, :] = hy.astype(BF16)
    pick = cell_ref[0].astype(BF16)
    at = cell_ref[1]
    lane = lanes(32, 128)
    packed = past_ref[...]
    for half in range(2):
        wide = jnp.zeros((32, 128), F32)
        for e in range(2):
            found = jnp.dot(pick, cells[2 * half + e], preferred_element_type=F32)
            value = jnp.sum(found * at, axis=1, keepdims=True)
            wide = jnp.where(lane == 64 * e + 63, value, wide)
        packed = packed + jnp.dot(
            select_ref[half].astype(BF16), wide.astype(BF16), preferred_element_type=F32
        )
    pack_out[0] = packed
    pack_out[1] = packed


def state_body(
    decay_ref, gain_ref, poles_ref, drive_ref, base_ref, slope_ref, h_ref, p_out, e_out, h_out
):
    decay = [decay_ref[0:1, p : p + 1] for p in range(poles_ref.shape[0])]
    gain = [gain_ref[0:1, p : p + 1] for p in range(poles_ref.shape[0])]
    for i in range(poles_ref.shape[2]):
        for comp in range(3):
            drive = drive_ref[comp, i]
            e_out[comp, i] = base_ref[comp, i] + slope_ref[i] * drive
            h_out[comp, i] = h_ref[comp, i]
            for p in range(poles_ref.shape[0]):
                p_out[p, comp, i] = decay[p] * poles_ref[p, comp, i] + gain[p] * drive


def pack_body(owner_ref, cell_ref, hist_ref, select_out, cell_out, pack_out):
    owner = owner_ref[...]
    onehot = jnp.where(rows(16, 32) == owner, 1.0, 0.0)
    earlier = jnp.where(rows(32, 32) < lanes(32, 32), 1.0, 0.0).astype(BF16)
    count = jnp.dot(onehot.astype(BF16), earlier, preferred_element_type=F32)
    rank = jnp.sum(count * onehot, axis=0, keepdims=True).astype(jnp.int32)
    slot = owner * 8 + rank
    cell = cell_ref[...]
    row = rows(128, 32)
    cell_out[0] = jnp.where(row == (cell >> 7), 1.0, 0.0).T
    cell_out[1] = jnp.where(row == (cell & 127), 1.0, 0.0).T
    packed = jnp.zeros((128, 128), F32)
    for half in range(2):
        select = jnp.where(row == slot + 4 * half, 1.0, 0.0)
        select_out[half] = select
        gap = jnp.zeros((32, 1), F32)
        past = [hist_ref[2 * half + e].astype(F32) for e in range(2)]
        past = jnp.concatenate([past[0], gap, past[1], gap], axis=1)
        packed = packed + jnp.dot(
            select.astype(BF16), past.astype(BF16), preferred_element_type=F32
        )
    pack_out[...] = packed


def project_body(core, got_ref, steer_ref, series_out, out_ref):
    got = got_ref[...].astype(BF16)
    row, slot = rows(256, 128), lanes(256, 128)
    parts = []
    for half in range(2):
        place = jnp.where(row == (slot >> 2) * 8 + 4 * half + (slot & 3), 1.0, 0.0).astype(BF16)
        moved = dot_t(got, place).astype(BF16)
        parts += [moved[:64], moved[64:]]
    series = jnp.concatenate(parts, axis=1)
    series_out[...] = series
    project_half(1 - core[0], series, steer_ref, out_ref, None)


def project_half(half, series, steer_ref, out_ref, add_ref):
    for n in range(4):
        first = pl.multiple_of(half * 1024 + n * 256, 256)
        part = jnp.dot(series, steer_ref[:, pl.ds(first, 256)], preferred_element_type=F32)
        for m in range(2):
            piece = part[:, m * 128 : (m + 1) * 128]
            out_ref[2 * n + m] = piece if add_ref is None else piece + add_ref[2 * n + m]


def project_own_body(core, series_ref, steer_ref, add_ref, out_ref):
    project_half(core[0], series_ref[...], steer_ref, out_ref, add_ref)


def sum_body(got_ref, out_ref):
    total = got_ref[0]
    for a in range(1, got_ref.shape[0]):
        total = total + got_ref[a]
    out_ref[...] = total


def spectrum_body(core, mine_ref, other_ref, table_ref, out_ref):
    mine, other = mine_ref[...], other_ref[...]
    first = core[0] == 0
    both = jnp.concatenate([jnp.where(first, mine, other), jnp.where(first, other, mine)], axis=0)
    high = both.astype(BF16)
    low = (both - high.astype(F32)).astype(BF16)
    out_ref[...] = jnp.dot(
        table_ref[core[0]], jnp.concatenate([high, low, high], axis=0), preferred_element_type=F32
    )


def finish_body(got_ref, out_ref):
    for g in range(8):
        total = got_ref[8 * g]
        for b in range(1, 8):
            total = total + got_ref[8 * g + b]
        for half in range(2):
            first = (8 * half + g) * 128
            for s in range(2):
                at = 4 * half + 2 * s
                out_ref[s, :, first : first + 128] = total[at : at + 2]


def spectral_table(steps):
    times = np.arange(steps, dtype=np.float64)
    levels = np.arange(FREQS, dtype=np.float64) + 0.5
    phase = math.pi / (2.0 * FREQS) * levels[:, None] * times[None, :]
    table = np.stack([np.cos(phase), -np.sin(phase)]) / math.sqrt(steps)
    return table.astype(np.float32)


def peer_table(steps):
    table = spectral_table(steps).reshape(2, 8, 2, 8, 2, steps).transpose(2, 1, 3, 0, 4, 5)
    wide = np.zeros((2, 8, 8, 2, 2, 2, 2, steps), np.float32)
    for half in range(2):
        wide[:, :, :, half, :, :, half, :] = table
    wide = wide.reshape(2, 512, 2 * steps)
    high = wide.astype(jnp.bfloat16)
    low = (wide - high.astype(np.float32)).astype(jnp.bfloat16)
    return jnp.asarray(np.concatenate([high, high, low], axis=2))


def shift(value, axis, step):
    count = lax.axis_size(axis)
    return lax.ppermute(value, axis, [(i, (i + step) % count) for i in range(count)])


def per_device(
    e_field, h_field, permittivity, wall_mask, poles, pole_decay, pole_gain, face_cells, owners,
    history, steering,
):
    nx, ny, nz = e_field.shape[1:]
    steps = history.shape[0] + 1
    axes = (GX, "gy", "gz")
    places = [lax.axis_index(axis) for axis in axes]
    keep = jnp.stack(
        [(at < lax.axis_size(axis) - 1) for at, axis in zip(places, axes)]
        + [at > 0 for at in places]
    ).astype(F32)
    core = lax.axis_index("core").reshape(1)
    block = struct(3, nx, ny, nz)
    faces = [struct(2, ny, nz), struct(2, nx, nz), struct(2, ny, 128)]

    *near, e_near, h_near = call(
        face_body, [*faces, block, block], [HB] * 2, [pltpu.SemaphoreType.DMA((2,))], data=400000
    )(far_off(e_field), far_off(h_field))
    up = [shift(face, axis, -1) for face, axis in zip(near, axes)]
    near, e_near, h_near = lax.optimization_barrier((near, e_near, h_near))
    later = [
        poles, permittivity, wall_mask, pole_decay.reshape(1, -1), pole_gain.reshape(1, -1),
        owners.reshape(1, -1), face_cells.reshape(1, -1), jnp.transpose(history, (1, 2, 0)),
    ]
    inner, poles, permittivity, wall_mask, decay, gain, owners, face_cells, history = call(
        inner_body,
        [block, *[struct(*value.shape, dtype=value.dtype) for value in later]],
        [VM] * 2 + [HB] * len(later),
        [pltpu.SemaphoreType.DMA((len(later),))],
        data=2600000,
    )(e_near, h_near, *[far_off(value) for value in later])

    h_mid, *far = call(mag_body, [block, *faces], [SM] + [VM] * 4, data=500000)(keep, inner, *up)
    down = [shift(face, axis, 1) for face, axis in zip(far, axes)]
    far, owners, poles = lax.optimization_barrier((far, owners, poles))
    select, cell, leaving = call(
        pack_body,
        [struct(2, 128, 32), struct(2, 32, 128), struct(128, 128)],
        [VM] * 3,
        data=200000,
    )(owners, face_cells, history)
    base, slope = call(wall_body, [block, struct(nx, ny, nz)], [VM] * 6, data=2400000)(
        decay, gain, poles, e_near, permittivity, wall_mask
    )

    drive, leaving = call(
        elec_body,
        [block, struct(2, 128, 128)],
        [SM] + [VM] * 9,
        scratch=[pltpu.VMEM((4, 128, 128), BF16)],
        data=1200000,
    )(keep, h_mid, *down, base, slope, select, cell, leaving)
    arrived = lax.all_to_all(leaving.reshape(32, 8, 128), ("gz", *GX), 0, 0, tiled=True)
    poles_next, e_next, h_next = call(
        state_body,
        [struct(*poles.shape), block, block],
        [VM] * 7,
        data=4500000,
    )(decay, gain, poles, drive, base, slope, h_mid)

    weights = steering.reshape(-1, steering.shape[2])
    series, part = call(
        project_body,
        [struct(64, 512, dtype=BF16), struct(8, 64, 128)],
        [SM] + [VM] * 2,
        flops=1 << 26,
        data=2600000,
    )(core, arrived.reshape(256, 128), weights)
    swap = [(0, 1), (1, 0)]
    part = lax.ppermute(part, "core", swap)
    series, poles_next = lax.optimization_barrier((series, poles_next))
    part = call(project_own_body, struct(8, 64, 128), [SM] + [VM] * 3, flops=1 << 26, data=2600000)(
        core, series, weights, part
    )
    part = lax.all_to_all(part, "gxc", 0, 0, tiled=True)
    mine = call(sum_body, struct(64, 128), [VM], data=300000)(part)
    other = lax.ppermute(mine, "core", swap)
    spectra = call(spectrum_body, struct(512, 128), [SM] + [VM] * 3, flops=1 << 27, data=900000)(
        core, mine, other, peer_table(steps)
    )
    spectra = lax.all_to_all(spectra.reshape(64, 8, 128), ("gxc", "gy"), 0, 0, tiled=True)
    far_field = call(finish_body, struct(2, 2, 2048), [VM], data=300000)(spectra)
    return (e_next, h_next, poles_next, far_field)


GX = ("gxc", "core")


def solution(mesh):
    shape = (mesh.shape["gx"] // 2, 2, mesh.shape["gy"], mesh.shape["gz"])
    mesh = jax.sharding.Mesh(mesh.devices.reshape(shape), ("gxc", "core", "gy", "gz"))
    return jax.shard_map(
        per_device,
        mesh=mesh,
        in_specs=(
            P(None, GX, "gy", "gz"),
            P(None, GX, "gy", "gz"),
            P(GX, "gy", "gz"),
            P(GX, "gy", "gz"),
            P(None, None, GX, "gy", "gz"),
            P(),
            P(),
            P((*GX, "gy", "gz")),
            P((*GX, "gy", "gz"), None),
            P(None, None, (*GX, "gy", "gz")),
            P(None, (*GX, "gy"), "gz"),
        ),
        out_specs=(
            P(None, GX, "gy", "gz"),
            P(None, GX, "gy", "gz"),
            P(None, None, GX, "gy", "gz"),
            P(None, (*GX, "gy"), "gz"),
        ),
        check_vma=False,
    )
```

time: 98 us -> 72.3 us (0.74)
  starting transfers between devices: 35.9 us -> 13.3 us
  blocking collectives: 28 us -> 44.4 us
  waiting for transfers between devices: 14 us -> 4.43 us
  local copies, waits for them, and re-layouts: 8.43 us -> 0.11 us
  Pallas kernels: 10.3 us -> 8.21 us
    all_to_all x3 -> x0, starting transfers between devices: 24.4 us -> none  [the longest x2 17.9 us: to_tiles(): lax.all_to_all(packed.reshape(32, 8, 128), ('gz', 'gx'), 0, 0, tiled=True)]
    all_to_all x2 -> x3, blocking collectives: 28 us -> 44.4 us  [the longest x1 17.8 us: per_device(): lax.all_to_all(spectra.reshape(64, 8, 128), ('gxc', 'gy'), 0, 0, tiled=True)]
    all_to_all x3 -> x0, waiting for transfers between devices: 11.7 us -> none  [the longest x2 6.96 us: to_tiles(): lax.all_to_all(packed.reshape(32, 8, 128), ('gz', 'gx'), 0, 0, tiled=True)]
    unnamed x32 -> x4, local copies, waits for them, and re-layouts: 7.43 us -> 0.01 us
    pallas_call x10 -> x12, Pallas kernels: 10.3 us -> 8.21 us  [the longest x1 1.55 us: per_device(): call(state_body, [struct(*poles.shape), block, block], [VM] * 7, data=450...]
    ppermute x6, waiting for transfers between devices: 2.24 us -> 3.57 us  [shift(): lax.ppermute(value, axis, [(i, (i + step) % count) for i in range(count)])]
    ppermute x0 -> x2, starting transfers between devices: none -> 1.31 us  [the longest x1 0.82 us: per_device(): other = lax.ppermute(mine, 'core', swap)]
  transfers between devices with their start and end apart: 9 -> 8, of which waited for: 4 -> 2; matrix products, arithmetic and copies ran while one was open for 0% -> 0% of each run, Pallas kernels for 7% -> 5%
where the time goes in v2:
time: 72.3 us; the launch traced here: 71.2 us
  blocking collectives  44.4 us (61%)
  starting transfers between devices  13.3 us (18%)
  Pallas kernels  8.21 us (11%)
  waiting for transfers between devices  4.43 us (6%)
  between operations  0.74 us (1%)
    all_to_all x1, blocking collectives, per_device(): lax.all_to_all(spectra.reshape(64, 8, 128), ('gxc', 'gy'), 0, 0, tiled=True)  17.8 us
    all_to_all x1, blocking collectives, per_device(): lax.all_to_all(leaving.reshape(32, 8, 128), ('gz', *GX), 0, 0, tiled=True)  16.7 us
    ppermute x6, starting transfers between devices, shift(): lax.ppermute(value, axis, [(i, (i + step) % count) for i in range(count)])  12 us
    all_to_all x1, blocking collectives, per_device(): part = lax.all_to_all(part, 'gxc', 0, 0, tiled=True)  9.91 us
    ppermute x6, waiting for transfers between devices, shift(): lax.ppermute(value, axis, [(i, (i + step) % count) for i in range(count)])  3.57 us
    pallas_call x1, Pallas kernels, per_device(): call(state_body, [struct(*poles.shape), block, block], [VM] * 7, data=450...  1.55 us
    pallas_call x1, Pallas kernels, per_device(): call(inner_body, [block, *[struct(*value.shape, dtype=value.dtype) for va...  1.49 us
  transfers between devices with their start and end apart: 8, of which 2 were waited for; matrix products, arithmetic and copies ran while one was open for 0% of the time, Pallas kernels for 5%

profile of v2, /device:TPU:1, one launch (start us, length us, event | category | flops | bytes accessed | tf_op | source)
XLA Modules:
  0.0 71.2 jit_solution(3882503911637303928)
XLA Ops:
  0.6 1.1 %shard_map.147 = (f32[2,16,128]{2,1,0:T(8,128)S(1)}, f32[2,8,128]{2,1,0:T(8,128)S(1)}, f32[2,16,128]{2,1,0:T(8,128)S(1)}, f32[3,8,16,128]{3,2,1,0:T(8,128)S(1)}, f32[3,8,16,128]{3,2,1,0:T(8,128)S(1)}) custom-call(f32[3,8,16,128]{3,2,1,0:T(8,128)} %e_far.1, f32[3,8,16,128]{3,2,1,0:T(8,128)} %h_far.1), custom_call_target="tpu_custom_call" | custom-call | bytes 400000 | tf_op jit(solution)/shard_map/pallas_call | solution.py:327
  1.7 3.3 %collective-permute-start = (f32[2,16,128]{2,1,0:T(8,128)S(1)}, f32[2,16,128]{2,1,0:T(8,128)S(1)}, u32[]{:S(2)}, u32[]{:S(2)}) collective-permute-start(f32[2,16,128]{2,1,0:T(8,128)S(1)} %get-tuple-element.49), channel_id=1, source_target_pairs={{0,240},{16,0},{32,16},{48,32},{64,48},{80,64},{96,80},{112,96},{1... | collective-permute-start | bytes 49160 | tf_op jit(solution)/shard_map/ppermute | solution.py:308
  5.0 1.2 %collective-permute-start.2 = (f32[2,16,128]{2,1,0:T(8,128)S(1)}, f32[2,16,128]{2,1,0:T(8,128)S(1)}, u32[]{:S(2)}, u32[]{:S(2)}) collective-permute-start(f32[2,16,128]{2,1,0:T(8,128)S(1)} %get-tuple-element.51), channel_id=1, source_target_pairs={{0,1},{1,0},{2,3},{3,2},{4,5},{5,4},{6,7},{7,6},{8,9},{9,8},{10,11... | collective-permute-start | bytes 49160 | tf_op jit(solution)/shard_map/ppermute | solution.py:308
  6.2 5.6 %collective-permute-start.1 = (f32[2,8,128]{2,1,0:T(8,128)S(1)}, f32[2,8,128]{2,1,0:T(8,128)S(1)}, u32[]{:S(2)}, u32[]{:S(2)}) collective-permute-start(f32[2,8,128]{2,1,0:T(8,128)S(1)} %get-tuple-element.50), channel_id=1, source_target_pairs={{0,14},{2,0},{4,2},{6,4},{8,6},{10,8},{12,10},{14,12},{1,15},{3,1}... | collective-permute-start | bytes 24584 | tf_op jit(solution)/shard_map/ppermute | solution.py:308
  11.8 0.1 stack.27
  11.9 1.5 %shard_map.148 = (f32[3,8,16,128]{3,2,1,0:T(8,128)S(1)}, f32[8,3,8,16,128]{4,3,2,1,0:T(8,128)S(1)}, f32[8,16,128]{2,1,0:T(8,128)S(1)}, s32[8,16,128]{2,1,0:T(8,1...) custom-call(f32[3,8,16,128]{3,2,1,0:T(8,128)S(1)} %get-tuple-element, ...), custom_call_target="tpu_custom_call" | custom-call | bytes 2600000 | tf_op jit(solution)/shard_map/pallas_call | solution.py:336
  13.4 0.7 %shard_map.149 = (f32[3,8,16,128]{3,2,1,0:T(8,128)S(1)}, f32[2,16,128]{2,1,0:T(8,128)S(1)}, f32[2,8,128]{2,1,0:T(8,128)S(1)}, f32[2,16,128]{2,1,0:T(8,128)S(1)}) custom-call(f32[6]{0:T(128)S(1)} %convert_element_type.3.keep, f32[3,8,16,128]{3,2,1,0:T(8,128)S(1)} %get-tuple-element.48.part_ref, f32[2,16,128]{2,1,0:T(8,128)S(1)} %collective-permute-done.ux_ref, ...), custom_call_target="tpu_custom_call" | custom-call | bytes 500000 | tf_op jit(solution)/shard_map/pallas_call | solution.py:344
  14.2 1.8 %collective-permute-start.3 = (f32[2,16,128]{2,1,0:T(8,128)S(1)}, f32[2,16,128]{2,1,0:T(8,128)S(1)}, u32[]{:S(2)}, u32[]{:S(2)}) collective-permute-start(f32[2,16,128]{2,1,0:T(8,128)S(1)} %get-tuple-element.52), channel_id=1, source_target_pairs={{0,16},{16,32},{32,48},{48,64},{64,80},{80,96},{96,112},{112,128},... | collective-permute-start | bytes 49160 | tf_op jit(solution)/shard_map/ppermute | solution.py:308
  16.0 0.1 collective-permute-start.5
  16.0 0.3 shard_map.151
  16.3 0.2 shard_map.150
  16.5 3.5 %collective-permute-done.4.dy_ref = f32[2,8,128]{2,1,0:T(8,128)S(1)} collective-permute-done((f32[2,8,128]{2,1,0:T(8,128)S(1)}, f32[2,8,128]{2,1,0:T(8,128)S(1)}, u32[]{:S(2)}, u32[]{:S(2)}) %collective-permute-start.4) | collective-permute-done | bytes 8224 | tf_op jit(solution)/shard_map/ppermute | solution.py:308
  20.1 1.2 %shard_map.152 = (f32[3,8,16,128]{3,2,1,0:T(8,128)S(1)}, f32[2,128,128]{2,1,0:T(8,128)S(1)}) custom-call(f32[6]{0:T(128)S(1)} %convert_element_type.3.keep, f32[3,8,16,128]{3,2,1,0:T(8,128)S(1)} %get-tuple-element.58.h_ref, f32[2,16,128]{2,1,0:T(8,128)S(1)} %collective-permute-done.3.dx_ref, f32[2,8,128]{2,1,0:T(8,128)S(1)} %collective-permute-done.4.dy_ref, ...), custom_call_target="tpu_custom_call" | custom-call | bytes 1200000 | tf_op jit(solution)/shard_map/pallas_call | solution.py:357
  21.3 16.7 %all_to_all.15 = f32[32,8,128]{2,1,0:T(8,128)S(1)} all-to-all(f32[32,8,128]{2,1,0:T(8,128)S(1)} %bitcast.20), channel_id=1, replica_groups=mesh['gxc'=8,'core'=2,'gy'=8,'gz'=2] {'gz','gxc','core'}, dimensions={0} | all-to-all | bytes 262144 | tf_op jit(solution)/shard_map/all_to_all | solution.py:364
  38.0 0.5 shard_map.154
  38.5 0.5 collective-permute-start.6
  39.0 1.5 %shard_map.153 = (f32[8,3,8,16,128]{4,3,2,1,0:T(8,128)}, f32[3,8,16,128]{3,2,1,0:T(8,128)}, f32[3,8,16,128]{3,2,1,0:T(8,128)}) custom-call(f32[1,8]{1,0:T(1,128)S(1)} %get-tuple-element.46.decay_ref, f32[1,8]{1,0:T(1,128)S(1)} %get-tuple-element.47.gain_ref, f32[8,3,8,16,128]{4,3,2,1,0:T(8,128)S(1)} %get-tuple-element.57.poles_ref, ...), custom_call_target="tpu_custom_call" | custom-call | bytes 4500000 | tf_op jit(solution)/shard_map/pallas_call | solution.py:365
  40.6 0.3 shard_map.155
  40.9 9.9 %all_to_all.16.got_ref = f32[8,64,128]{2,1,0:T(8,128)S(1)} all-to-all(f32[8,64,128]{2,1,0:T(8,128)S(1)} %shard_map.155), channel_id=1, replica_groups=mesh['gxc'=8,'core'=2,'gy'=8,'gz'=2] {'gxc'}, dimensions={0} | all-to-all | bytes 524288 | tf_op jit(solution)/shard_map/all_to_all | solution.py:386
  50.8 0.8 %collective-permute-start.7 = (f32[64,128]{1,0:T(8,128)S(1)}, f32[64,128]{1,0:T(8,128)S(1)}, u32[]{:S(2)}, u32[]{:S(2)}) collective-permute-start(f32[64,128]{1,0:T(8,128)S(1)} %shard_map.156.mine_ref), channel_id=1, source_target_pairs={{0,16},{16,0},{1,17},{17,1},{2,18},{18,2},{3,19},{19,3},{4,20},{20... | collective-permute-start | bytes 98312 | tf_op jit(solution)/shard_map/ppermute | solution.py:388
  51.6 0.9 %collective-permute-done.7.other_ref = f32[64,128]{1,0:T(8,128)S(1)} collective-permute-done((f32[64,128]{1,0:T(8,128)S(1)}, f32[64,128]{1,0:T(8,128)S(1)}, u32[]{:S(2)}, u32[]{:S(2)}) %collective-permute-start.7) | collective-permute-done | bytes 32800 | tf_op jit(solution)/shard_map/ppermute | solution.py:388
  52.5 0.3 shard_map.157
  52.8 17.8 %all_to_all.17.got_ref = f32[64,8,128]{2,1,0:T(8,128)S(1)} all-to-all(f32[64,8,128]{2,1,0:T(8,128)S(1)} %bitcast.18), channel_id=1, replica_groups=mesh['gxc'=8,'core'=2,'gy'=8,'gz'=2] {'gxc','gy'}, dimensions={0} | all-to-all | bytes 524288 | tf_op jit(solution)/shard_map/all_to_all | solution.py:392
  70.5 0.6 shard_map.158
  (13 shorter events, 0.1 us)
Async XLA Ops:
  1.7 11.7 %collective-permute-start = (f32[2,16,128]{2,1,0:T(8,128)S(1)}, f32[2,16,128]{2,1,0:T(8,128)S(1)}, u32[]{:S(2)}, u32[]{:S(2)}) collective-permute-start(f32[2,16,128]{2,1,0:T(8,128)S(1)} %get-tuple-element.49), channel_id=1, source_target_pairs={{0,240},{16,0},{32,16},{48,32},{64,48},{80,64},{96,80},{112,96},{1... | collective-permute-start | bytes 49160 | tf_op jit(solution)/shard_map/ppermute | solution.py:308
  5.0 8.4 %collective-permute-start.2 = (f32[2,16,128]{2,1,0:T(8,128)S(1)}, f32[2,16,128]{2,1,0:T(8,128)S(1)}, u32[]{:S(2)}, u32[]{:S(2)}) collective-permute-start(f32[2,16,128]{2,1,0:T(8,128)S(1)} %get-tuple-element.51), channel_id=1, source_target_pairs={{0,1},{1,0},{2,3},{3,2},{4,5},{5,4},{6,7},{7,6},{8,9},{9,8},{10,11... | collective-permute-start | bytes 49160 | tf_op jit(solution)/shard_map/ppermute | solution.py:308
  6.2 7.2 %collective-permute-start.1 = (f32[2,8,128]{2,1,0:T(8,128)S(1)}, f32[2,8,128]{2,1,0:T(8,128)S(1)}, u32[]{:S(2)}, u32[]{:S(2)}) collective-permute-start(f32[2,8,128]{2,1,0:T(8,128)S(1)} %get-tuple-element.50), channel_id=1, source_target_pairs={{0,14},{2,0},{4,2},{6,4},{8,6},{10,8},{12,10},{14,12},{1,15},{3,1}... | collective-permute-start | bytes 24584 | tf_op jit(solution)/shard_map/ppermute | solution.py:308
  13.4 24.6 %copy-start = (bf16[4,128,2048]{2,1,0:T(8,128)(2,1)S(1)}, bf16[4,128,2048]{2,1,0:T(8,128)(2,1)}, u32[]{:S(2)}) copy-start(bf16[4,128,2048]{2,1,0:T(8,128)(2,1)} %param.22) | copy-start | bytes 6291460
  14.2 5.9 %collective-permute-start.3 = (f32[2,16,128]{2,1,0:T(8,128)S(1)}, f32[2,16,128]{2,1,0:T(8,128)S(1)}, u32[]{:S(2)}, u32[]{:S(2)}) collective-permute-start(f32[2,16,128]{2,1,0:T(8,128)S(1)} %get-tuple-element.52), channel_id=1, source_target_pairs={{0,16},{16,32},{32,48},{48,64},{64,80},{80,96},{96,112},{112,128},... | collective-permute-start | bytes 49160 | tf_op jit(solution)/shard_map/ppermute | solution.py:308
  16.0 4.1 %collective-permute-start.5 = (f32[2,16,128]{2,1,0:T(8,128)S(1)}, f32[2,16,128]{2,1,0:T(8,128)S(1)}, u32[]{:S(2)}, u32[]{:S(2)}) collective-permute-start(f32[2,16,128]{2,1,0:T(8,128)S(1)} %get-tuple-element.54), channel_id=1, source_target_pairs={{0,1},{1,0},{2,3},{3,2},{4,5},{5,4},{6,7},{7,6},{8,9},{9,8},{10,11... | collective-permute-start | bytes 49160 | tf_op jit(solution)/shard_map/ppermute | solution.py:308
  16.0 4.0 %collective-permute-start.4 = (f32[2,8,128]{2,1,0:T(8,128)S(1)}, f32[2,8,128]{2,1,0:T(8,128)S(1)}, u32[]{:S(2)}, u32[]{:S(2)}) collective-permute-start(f32[2,8,128]{2,1,0:T(8,128)S(1)} %get-tuple-element.53), channel_id=1, source_target_pairs={{0,2},{2,4},{4,6},{6,8},{8,10},{10,12},{12,14},{14,0},{1,3},{3,5},... | collective-permute-start | bytes 24584 | tf_op jit(solution)/shard_map/ppermute | solution.py:308
  38.5 2.0 %collective-permute-start.6 = (f32[8,64,128]{2,1,0:T(8,128)S(1)}, f32[8,64,128]{2,1,0:T(8,128)S(1)}, u32[]{:S(2)}, u32[]{:S(2)}) collective-permute-start(f32[8,64,128]{2,1,0:T(8,128)S(1)} %get-tuple-element.77), channel_id=1, source_target_pairs={{0,16},{16,0},{1,17},{17,1},{2,18},{18,2},{3,19},{19,3},{4,20},{20... | collective-permute-start | bytes 786440 | tf_op jit(solution)/shard_map/ppermute | solution.py:381
  40.6 11.9 %copy-start.1 = (bf16[2,512,384]{2,1,0:T(8,128)(2,1)S(1)}, bf16[2,512,384]{2,1,0:T(8,128)(2,1)}, u32[]{:S(2)}) copy-start(bf16[2,512,384]{2,1,0:T(8,128)(2,1)} %constant.28.clone.table_ref) | copy-start | bytes 2359300
  50.8 1.7 %collective-permute-start.7 = (f32[64,128]{1,0:T(8,128)S(1)}, f32[64,128]{1,0:T(8,128)S(1)}, u32[]{:S(2)}, u32[]{:S(2)}) collective-permute-start(f32[64,128]{1,0:T(8,128)S(1)} %shard_map.156.mine_ref), channel_id=1, source_target_pairs={{0,16},{16,0},{1,17},{17,1},{2,18},{18,2},{3,19},{19,3},{4,20},{20... | collective-permute-start | bytes 98312 | tf_op jit(solution)/shard_map/ppermute | solution.py:388

commit v3 on v2

--- a/solution.py
+++ b/solution.py
@@ -63,6 +63,7 @@
     fx_ref[0] = e_ref[1, 0]
     fx_ref[1] = e_ref[2, 0]
     lane = lanes(16, 128)
+    fy_ref[...] = jnp.zeros_like(fy_ref)
     for part, comp in enumerate((0, 2)):
         for i in range(nx):
             fy_ref[part, i : i + 1, :] = e_ref[comp, i, 0:1, :]
@@ -71,7 +72,8 @@
         for i in range(nx):
             moved = e_ref[comp, i] if i == 0 else pltpu.roll(e_ref[comp, i], i, 1)
             acc = jnp.where(lane == i, moved, acc)
-        fz_ref[part] = acc
+        fz_ref[part, 0:16, :] = acc
+        fz_ref[part, 16:24, :] = jnp.zeros((8, 128), F32)
     bring[1].wait()
 
 
@@ -104,8 +106,9 @@
     row = rows(16, 128)
     up_x = [ux_ref[part] * (0.5 * keep[0]) for part in range(2)]
     up_y = [uy_ref[part] * (0.5 * keep[1]) for part in range(2)]
-    up_z = [uz_ref[part] * (0.5 * keep[2]) for part in range(2)]
+    up_z = [uz_ref[part, 0:16, :] * (0.5 * keep[2]) for part in range(2)]
     face_z = [jnp.zeros((16, 128), F32), jnp.zeros((16, 128), F32)]
+    gy_ref[...] = jnp.zeros_like(gy_ref)
     for i in range(nx):
         ex_z, ey_z = [jnp.where(lane == 127, pltpu.roll(v, 127 - i, 1), 0.0) for v in up_z]
         ex_y, ez_y = [jnp.where(row == 15, v[i : i + 1], 0.0) for v in up_y]
@@ -124,8 +127,9 @@
         gy_ref[1, i : i + 1, :] = hz[15:16]
         for part, value in enumerate((hx, hy)):
             face_z[part] = jnp.where(lane == i, pltpu.roll(value, i + 1, 1), face_z[part])
-    gz_ref[0] = face_z[0]
-    gz_ref[1] = face_z[1]
+    for part in range(2):
+        gz_ref[part, 0:16, :] = face_z[part]
+        gz_ref[part, 16:24, :] = jnp.zeros((8, 128), F32)
 
 
 def wall_body(decay_ref, gain_ref, poles_ref, e_ref, eps_ref, wall_ref, base_out, slope_out):
@@ -150,7 +154,7 @@
     row = rows(16, 128)
     dn_x = [dx_ref[part] * keep[3] for part in range(2)]
     dn_y = [dy_ref[part] * keep[4] for part in range(2)]
-    dn_z = [dz_ref[part] * keep[5] for part in range(2)]
+    dn_z = [dz_ref[part, 0:16, :] * keep[5] for part in range(2)]
     for i in range(nx):
         hx, hy, hz = h_ref[0, i], h_ref[1, i], h_ref[2, i]
         hy_x = h_ref[1, i - 1] if i else dn_x[0]
@@ -171,40 +175,42 @@
         for comp in range(2):
             field = base_ref[comp, i] + slope_ref[i] * drive[comp]
             cells[comp, span, :] = field.astype(BF16)
-        cells[2, span, :] = hx.astype(BF16)
-        cells[3, span, :] = hy.astype(BF16)
-    pick = cell_ref[0].astype(BF16)
-    at = cell_ref[1]
-    lane = lanes(32, 128)
-    packed = past_ref[...]
-    for half in range(2):
-        wide = jnp.zeros((32, 128), F32)
-        for e in range(2):
-            found = jnp.dot(pick, cells[2 * half + e], preferred_element_type=F32)
-            value = jnp.sum(found * at, axis=1, keepdims=True)
-            wide = jnp.where(lane == 64 * e + 63, value, wide)
-        packed = packed + jnp.dot(
-            select_ref[half].astype(BF16), wide.astype(BF16), preferred_element_type=F32
-        )
+    packed = past_ref[...] + picked(cells, select_ref[0], cell_ref[0], cell_ref[1])
+    packed = packed.astype(BF16)
     pack_out[0] = packed
     pack_out[1] = packed
 
 
-def state_body(
-    decay_ref, gain_ref, poles_ref, drive_ref, base_ref, slope_ref, h_ref, p_out, e_out, h_out
-):
+def picked(cells, select, pick, at):
+    lane = lanes(32, 128)
+    wide = jnp.zeros((32, 128), F32)
+    for e in range(2):
+        found = jnp.dot(pick.astype(BF16), cells[e], preferred_element_type=F32)
+        value = jnp.sum(found * at, axis=1, keepdims=True)
+        wide = jnp.where(lane == 64 * e + 63, value, wide)
+    return jnp.dot(select.astype(BF16), wide.astype(BF16), preferred_element_type=F32)
+
+
+def poles_body(decay_ref, gain_ref, poles_ref, drive_ref, out_ref):
     decay = [decay_ref[0:1, p : p + 1] for p in range(poles_ref.shape[0])]
     gain = [gain_ref[0:1, p : p + 1] for p in range(poles_ref.shape[0])]
     for i in range(poles_ref.shape[2]):
         for comp in range(3):
             drive = drive_ref[comp, i]
-            e_out[comp, i] = base_ref[comp, i] + slope_ref[i] * drive
-            h_out[comp, i] = h_ref[comp, i]
             for p in range(poles_ref.shape[0]):
-                p_out[p, comp, i] = decay[p] * poles_ref[p, comp, i] + gain[p] * drive
-
-
-def pack_body(owner_ref, cell_ref, hist_ref, select_out, cell_out, pack_out):
+                out_ref[p, comp, i] = decay[p] * poles_ref[p, comp, i] + gain[p] * drive
+
+
+def field_body(drive_ref, base_ref, slope_ref, h_ref, e_out, h_out):
+    h_out[...] = h_ref[...]
+    for comp in range(3):
+        e_out[comp] = base_ref[comp] + slope_ref[...] * drive_ref[comp]
+
+
+def pack_body(owner_ref, cell_ref, hist_ref, h_ref, select_out, cell_out, pack_out, cells):
+    for comp in range(2):
+        for i in range(h_ref.shape[1]):
+            cells[comp, i * 16 : (i + 1) * 16, :] = h_ref[comp, i].astype(BF16)
     owner = owner_ref[...]
     onehot = jnp.where(rows(16, 32) == owner, 1.0, 0.0)
     earlier = jnp.where(rows(32, 32) < lanes(32, 32), 1.0, 0.0).astype(BF16)
@@ -213,8 +219,10 @@
     slot = owner * 8 + rank
     cell = cell_ref[...]
     row = rows(128, 32)
-    cell_out[0] = jnp.where(row == (cell >> 7), 1.0, 0.0).T
-    cell_out[1] = jnp.where(row == (cell & 127), 1.0, 0.0).T
+    pick = jnp.where(row == (cell >> 7), 1.0, 0.0).T
+    at = jnp.where(row == (cell & 127), 1.0, 0.0).T
+    cell_out[0] = pick
+    cell_out[1] = at
     packed = jnp.zeros((128, 128), F32)
     for half in range(2):
         select = jnp.where(row == slot + 4 * half, 1.0, 0.0)
@@ -225,11 +233,19 @@
         packed = packed + jnp.dot(
             select.astype(BF16), past.astype(BF16), preferred_element_type=F32
         )
-    pack_out[...] = packed
+    pack_out[...] = packed + picked(cells, select, pick, at)
+
+
+def beside(first, second):
+    low = lanes(*first.shape) < 64
+    return (
+        jnp.where(low, first, pltpu.roll(second, 64, 1)),
+        jnp.where(low, pltpu.roll(first, 64, 1), second),
+    )
 
 
 def project_body(core, got_ref, steer_ref, series_out, out_ref):
-    got = got_ref[...].astype(BF16)
+    got = got_ref[...]
     row, slot = rows(256, 128), lanes(256, 128)
     parts = []
     for half in range(2):
@@ -246,8 +262,10 @@
         first = pl.multiple_of(half * 1024 + n * 256, 256)
         part = jnp.dot(series, steer_ref[:, pl.ds(first, 256)], preferred_element_type=F32)
         for m in range(2):
-            piece = part[:, m * 128 : (m + 1) * 128]
-            out_ref[2 * n + m] = piece if add_ref is None else piece + add_ref[2 * n + m]
+            pair = beside(part[:32, m * 128 : (m + 1) * 128], part[32:, m * 128 : (m + 1) * 128])
+            for y in range(2):
+                at = 4 * n + 2 * m + y
+                out_ref[at] = pair[y] if add_ref is None else pair[y] + add_ref[at]
 
 
 def project_own_body(core, series_ref, steer_ref, add_ref, out_ref):
@@ -264,7 +282,8 @@
 def spectrum_body(core, mine_ref, other_ref, table_ref, out_ref):
     mine, other = mine_ref[...], other_ref[...]
     first = core[0] == 0
-    both = jnp.concatenate([jnp.where(first, mine, other), jnp.where(first, other, mine)], axis=0)
+    both = beside(jnp.where(first, mine, other), jnp.where(first, other, mine))
+    both = jnp.concatenate(both, axis=0)
     high = both.astype(BF16)
     low = (both - high.astype(F32)).astype(BF16)
     out_ref[...] = jnp.dot(
@@ -273,15 +292,15 @@
 
 
 def finish_body(got_ref, out_ref):
-    for g in range(8):
-        total = got_ref[8 * g]
-        for b in range(1, 8):
-            total = total + got_ref[8 * g + b]
-        for half in range(2):
-            first = (8 * half + g) * 128
+    total = [got_ref[32 * y : 32 * y + 32, :] for y in range(2)]
+    for b in range(1, 4):
+        total = [total[y] + got_ref[64 * b + 32 * y : 64 * b + 32 * y + 32, :] for y in range(2)]
+    for core, value in enumerate(beside(*total)):
+        for g in range(8):
+            first = (8 * core + g) * 128
             for s in range(2):
-                at = 4 * half + 2 * s
-                out_ref[s, :, first : first + 128] = total[at : at + 2]
+                at = 4 * g + 2 * s
+                out_ref[s, :, first : first + 128] = value[at : at + 2]
 
 
 def spectral_table(steps):
@@ -293,19 +312,24 @@
 
 
 def peer_table(steps):
-    table = spectral_table(steps).reshape(2, 8, 2, 8, 2, steps).transpose(2, 1, 3, 0, 4, 5)
-    wide = np.zeros((2, 8, 8, 2, 2, 2, 2, steps), np.float32)
-    for half in range(2):
-        wide[:, :, :, half, :, :, half, :] = table
-    wide = wide.reshape(2, 512, 2 * steps)
-    high = wide.astype(jnp.bfloat16)
-    low = (wide - high.astype(np.float32)).astype(jnp.bfloat16)
+    table = spectral_table(steps).reshape(2, 8, 2, 8, 2, steps).transpose(2, 3, 1, 0, 4, 5)
+    table = table.reshape(2, 256, steps)
+    high = table.astype(jnp.bfloat16)
+    low = (table - high.astype(np.float32)).astype(jnp.bfloat16)
     return jnp.asarray(np.concatenate([high, high, low], axis=2))
 
 
 def shift(value, axis, step):
     count = lax.axis_size(axis)
     return lax.ppermute(value, axis, [(i, (i + step) % count) for i in range(count)])
+
+
+def cross(sender):
+    pairs, count = [], lax.axis_size("gxc")
+    for g in range(count):
+        near = (g + count // 2) % count
+        pairs += [(2 * g + sender, 2 * g + 1 - sender), (2 * g + 1 - sender, 2 * near + sender)]
+    return pairs
 
 
 def per_device(
@@ -314,7 +338,7 @@
 ):
     nx, ny, nz = e_field.shape[1:]
     steps = history.shape[0] + 1
-    axes = (GX, "gy", "gz")
+    axes = (GX, GY, "gz")
     places = [lax.axis_index(axis) for axis in axes]
     keep = jnp.stack(
         [(at < lax.axis_size(axis) - 1) for at, axis in zip(places, axes)]
@@ -322,12 +346,14 @@
     ).astype(F32)
     core = lax.axis_index("core").reshape(1)
     block = struct(3, nx, ny, nz)
-    faces = [struct(2, ny, nz), struct(2, nx, nz), struct(2, ny, 128)]
+    faces = [struct(2, ny, nz), struct(2, 4 * nx, nz), struct(2, ny + 8, 128)]
+    faces_up = [struct(2, ny, nz), struct(2, nx, nz), struct(2, ny + 8, 128)]
 
     *near, e_near, h_near = call(
         face_body, [*faces, block, block], [HB] * 2, [pltpu.SemaphoreType.DMA((2,))], data=400000
     )(far_off(e_field), far_off(h_field))
-    up = [shift(face, axis, -1) for face, axis in zip(near, axes)]
+    up = [shift(face, axis, -1) for face, axis in zip(near[:2], axes)]
+    up.append(lax.ppermute(near[2], ("gxc", "gz"), cross(1)))
     near, e_near, h_near = lax.optimization_barrier((near, e_near, h_near))
     later = [
         poles, permittivity, wall_mask, pole_decay.reshape(1, -1), pole_gain.reshape(1, -1),
@@ -341,86 +367,89 @@
         data=2600000,
     )(e_near, h_near, *[far_off(value) for value in later])
 
-    h_mid, *far = call(mag_body, [block, *faces], [SM] + [VM] * 4, data=500000)(keep, inner, *up)
-    down = [shift(face, axis, 1) for face, axis in zip(far, axes)]
+    h_mid, *far = call(mag_body, [block, *faces_up], [SM] + [VM] * 4, data=500000)(keep, inner, *up)
+    down = [shift(face, axis, 1) for face, axis in zip(far[:2], axes)]
+    down.append(lax.ppermute(far[2], ("gxc", "gz"), cross(0)))
     far, owners, poles = lax.optimization_barrier((far, owners, poles))
     select, cell, leaving = call(
         pack_body,
         [struct(2, 128, 32), struct(2, 32, 128), struct(128, 128)],
-        [VM] * 3,
+        [VM] * 4,
+        scratch=[pltpu.VMEM((2, 128, 128), BF16)],
         data=200000,
-    )(owners, face_cells, history)
+    )(owners, face_cells, history, h_mid)
     base, slope = call(wall_body, [block, struct(nx, ny, nz)], [VM] * 6, data=2400000)(
         decay, gain, poles, e_near, permittivity, wall_mask
     )
 
     drive, leaving = call(
         elec_body,
-        [block, struct(2, 128, 128)],
+        [block, struct(2, 128, 128, dtype=BF16)],
         [SM] + [VM] * 9,
-        scratch=[pltpu.VMEM((4, 128, 128), BF16)],
+        scratch=[pltpu.VMEM((2, 128, 128), BF16)],
         data=1200000,
     )(keep, h_mid, *down, base, slope, select, cell, leaving)
     arrived = lax.all_to_all(leaving.reshape(32, 8, 128), ("gz", *GX), 0, 0, tiled=True)
-    poles_next, e_next, h_next = call(
-        state_body,
-        [struct(*poles.shape), block, block],
-        [VM] * 7,
-        data=4500000,
-    )(decay, gain, poles, drive, base, slope, h_mid)
+    poles_next = call(poles_body, struct(*poles.shape), [VM] * 4, data=3400000)(
+        decay, gain, poles, drive
+    )
+    e_next, h_next = call(field_body, [block, block], [VM] * 4, data=1200000)(
+        drive, base, slope, h_mid
+    )
 
     weights = steering.reshape(-1, steering.shape[2])
     series, part = call(
         project_body,
-        [struct(64, 512, dtype=BF16), struct(8, 64, 128)],
+        [struct(64, 512, dtype=BF16), struct(16, 32, 128)],
         [SM] + [VM] * 2,
         flops=1 << 26,
         data=2600000,
     )(core, arrived.reshape(256, 128), weights)
-    swap = [(0, 1), (1, 0)]
-    part = lax.ppermute(part, "core", swap)
+    part = lax.ppermute(part, "core", [(0, 1), (1, 0)])
     series, poles_next = lax.optimization_barrier((series, poles_next))
-    part = call(project_own_body, struct(8, 64, 128), [SM] + [VM] * 3, flops=1 << 26, data=2600000)(
+    part = call(project_own_body, struct(16, 32, 128), [SM] + [VM] * 3, flops=1 << 26, data=2600000)(
         core, series, weights, part
     )
-    part = lax.all_to_all(part, "gxc", 0, 0, tiled=True)
-    mine = call(sum_body, struct(64, 128), [VM], data=300000)(part)
-    other = lax.ppermute(mine, "core", swap)
-    spectra = call(spectrum_body, struct(512, 128), [SM] + [VM] * 3, flops=1 << 27, data=900000)(
+    part = lax.all_to_all(part, ("gxc", "gyl"), 0, 0, tiled=True)
+    mine = call(sum_body, struct(32, 128), [VM], data=300000)(part)
+    other = lax.ppermute(mine, "core", [(0, 1), (1, 0)])
+    core, e_next = lax.optimization_barrier((core, e_next))
+    spectra = call(spectrum_body, struct(256, 128), [SM] + [VM] * 3, flops=1 << 27, data=900000)(
         core, mine, other, peer_table(steps)
     )
-    spectra = lax.all_to_all(spectra.reshape(64, 8, 128), ("gxc", "gy"), 0, 0, tiled=True)
+    spectra = lax.all_to_all(spectra, (*GY, "gxc"), 0, 0, tiled=True)
     far_field = call(finish_body, struct(2, 2, 2048), [VM], data=300000)(spectra)
     return (e_next, h_next, poles_next, far_field)
 
 
 GX = ("gxc", "core")
+GY = ("gyh", "gyl")
 
 
 def solution(mesh):
-    shape = (mesh.shape["gx"] // 2, 2, mesh.shape["gy"], mesh.shape["gz"])
-    mesh = jax.sharding.Mesh(mesh.devices.reshape(shape), ("gxc", "core", "gy", "gz"))
+    shape = (mesh.shape["gx"] // 2, 2, mesh.shape["gy"] // 2, 2, mesh.shape["gz"])
+    mesh = jax.sharding.Mesh(mesh.devices.reshape(shape), (*GX, *GY, "gz"))
     return jax.shard_map(
         per_device,
         mesh=mesh,
         in_specs=(
-            P(None, GX, "gy", "gz"),
-            P(None, GX, "gy", "gz"),
-            P(GX, "gy", "gz"),
-            P(GX, "gy", "gz"),
-            P(None, None, GX, "gy", "gz"),
+            P(None, GX, GY, "gz"),
+            P(None, GX, GY, "gz"),
+            P(GX, GY, "gz"),
+            P(GX, GY, "gz"),
+            P(None, None, GX, GY, "gz"),
             P(),
             P(),
-            P((*GX, "gy", "gz")),
-            P((*GX, "gy", "gz"), None),
-            P(None, None, (*GX, "gy", "gz")),
-            P(None, (*GX, "gy"), "gz"),
+            P((*GX, *GY, "gz")),
+            P((*GX, *GY, "gz"), None),
+            P(None, None, (*GX, *GY, "gz")),
+            P(None, (*GX, *GY), "gz"),
         ),
         out_specs=(
-            P(None, GX, "gy", "gz"),
-            P(None, GX, "gy", "gz"),
-            P(None, None, GX, "gy", "gz"),
-            P(None, (*GX, "gy"), "gz"),
+            P(None, GX, GY, "gz"),
+            P(None, GX, GY, "gz"),
+            P(None, None, GX, GY, "gz"),
+            P(None, (*GX, *GY), "gz"),
         ),
         check_vma=False,
     )

time: 72.3 us -> 67.8 us (0.938); the launches traced: 71.2 us -> 67.6 us
  blocking collectives: 44.4 us -> 38.6 us
  starting transfers between devices: 13.3 us -> 15 us
  Pallas kernels: 8.21 us -> 9.12 us
    ppermute x2 -> x4, starting transfers between devices: 1.31 us -> 4.97 us  [the longest x1 2.73 us: per_device(): up.append(lax.ppermute(near[2], ('gxc', 'gz'), cross(1)))]
    all_to_all x2, blocking collectives: 27.7 us -> 24.3 us  [the longest x1 15 us: per_device(): spectra = lax.all_to_all(spectra, (*GY, 'gxc'), 0, 0, tiled=True)]
    all_to_all x1, blocking collectives: 16.7 us -> 14.3 us  [per_device(): lax.all_to_all(leaving.reshape(32, 8, 128), ('gz', *GX), 0, 0, tiled=True)]
    ppermute x6 -> x4, starting transfers between devices: 12 us -> 10.1 us  [shift(): lax.ppermute(value, axis, [(i, (i + step) % count) for i in range(count)])]
    ppermute x2 -> x4, waiting for transfers between devices: 0.86 us -> 0.06 us  [the longest x1 0.05 us: per_device(): other = lax.ppermute(mine, 'core', [(0, 1), (1, 0)])]
    pallas_call x7 -> x8, Pallas kernels: 4.57 us -> 5.17 us  [the longest x1 1.44 us: per_device(): call(poles_body, struct(*poles.shape), [VM] * 4, data=3400000)]
    ppermute x6 -> x4, waiting for transfers between devices: 3.57 us -> 3.9 us  [shift(): lax.ppermute(value, axis, [(i, (i + step) % count) for i in range(count)])]
  transfers between devices with their start and end apart: 8 -> 8, of which waited for: 2 -> 3; matrix products, arithmetic and copies ran while one was open for 0% -> 0% of each run, Pallas kernels for 5% -> 7%
where the time goes in v3:
time: 67.8 us; the launch traced here: 67.6 us
  blocking collectives  38.6 us (57%)
  starting transfers between devices  15 us (22%)
  Pallas kernels  9.12 us (13%)
  waiting for transfers between devices  3.96 us (6%)
  between operations  0.72 us (1%)
    all_to_all x1, blocking collectives, per_device(): spectra = lax.all_to_all(spectra, (*GY, 'gxc'), 0, 0, tiled=True)  15 us
    all_to_all x1, blocking collectives, per_device(): lax.all_to_all(leaving.reshape(32, 8, 128), ('gz', *GX), 0, 0, tiled=True)  14.3 us
    ppermute x4, starting transfers between devices, shift(): lax.ppermute(value, axis, [(i, (i + step) % count) for i in range(count)])  10.1 us
    all_to_all x1, blocking collectives, per_device(): part = lax.all_to_all(part, ('gxc', 'gyl'), 0, 0, tiled=True)  9.29 us
    ppermute x4, waiting for transfers between devices, shift(): lax.ppermute(value, axis, [(i, (i + step) % count) for i in range(count)])  3.9 us
    ppermute x1, starting transfers between devices, per_device(): up.append(lax.ppermute(near[2], ('gxc', 'gz'), cross(1)))  2.73 us
    pallas_call x1, Pallas kernels, per_device(): call(inner_body, [block, *[struct(*value.shape, dtype=value.dtype) for va...  1.49 us
    ppermute x1, starting transfers between devices, per_device(): other = lax.ppermute(mine, 'core', [(0, 1), (1, 0)])  1.44 us
  transfers between devices with their start and end apart: 8, of which 3 were waited for; matrix products, arithmetic and copies ran while one was open for 0% of the time, Pallas kernels for 7%

profile of v3, /device:TPU:1, one launch (start us, length us, event | category | flops | bytes accessed | tf_op | source)
XLA Modules:
  0.0 67.6 jit_solution(7190567182107711976)
XLA Ops:
  0.6 1.1 %shard_map.147 = (f32[2,16,128]{2,1,0:T(8,128)S(1)}, f32[2,32,128]{2,1,0:T(8,128)S(1)}, f32[2,24,128]{2,1,0:T(8,128)S(1)}, f32[3,8,16,128]{3,2,1,0:T(8,128)S(1)}, f32[3,8,16,128]{3,2,1,0:T(8,128)S(1)}) custom-call(f32[3,8,16,128]{3,2,1,0:T(8,128)} %e_far.1, f32[3,8,16,128]{3,2,1,0:T(8,128)} %h_far.1), custom_call_target="tpu_custom_call" | custom-call | bytes 400000 | tf_op jit(solution)/shard_map/pallas_call | solution.py:352
  1.7 6.5 %collective-permute-start.1 = (f32[2,32,128]{2,1,0:T(8,128)S(1)}, f32[2,32,128]{2,1,0:T(8,128)S(1)}, u32[]{:S(2)}, u32[]{:S(2)}) collective-permute-start(f32[2,32,128]{2,1,0:T(8,128)S(1)} %get-tuple-element.49), channel_id=1, source_target_pairs={{0,14},{2,0},{4,2},{6,4},{8,6},{10,8},{12,10},{14,12},{1,15},{3,1}... | collective-permute-start | bytes 98312 | tf_op jit(solution)/shard_map/ppermute | solution.py:324
  8.2 2.7 %collective-permute-start.2 = (f32[2,24,128]{2,1,0:T(8,128)S(1)}, f32[2,24,128]{2,1,0:T(8,128)S(1)}, u32[]{:S(2)}, u32[]{:S(2)}) collective-permute-start(f32[2,24,128]{2,1,0:T(8,128)S(1)} %get-tuple-element.50), channel_id=1, source_target_pairs={{1,0},{0,129},{33,32},{32,161},{65,64},{64,193},{97,96},{96,225},{... | collective-permute-start | bytes 73736 | tf_op jit(solution)/shard_map/ppermute | solution.py:356
  10.9 1.2 %collective-permute-start = (f32[2,16,128]{2,1,0:T(8,128)S(1)}, f32[2,16,128]{2,1,0:T(8,128)S(1)}, u32[]{:S(2)}, u32[]{:S(2)}) collective-permute-start(f32[2,16,128]{2,1,0:T(8,128)S(1)} %get-tuple-element.48), channel_id=1, source_target_pairs={{0,240},{16,0},{32,16},{48,32},{64,48},{80,64},{96,80},{112,96},{1... | collective-permute-start | bytes 49160 | tf_op jit(solution)/shard_map/ppermute | solution.py:324
  12.3 1.5 %shard_map.148 = (f32[3,8,16,128]{3,2,1,0:T(8,128)S(1)}, f32[8,3,8,16,128]{4,3,2,1,0:T(8,128)S(1)}, f32[8,16,128]{2,1,0:T(8,128)S(1)}, s32[8,16,128]{2,1,0:T(8,1...) custom-call(f32[3,8,16,128]{3,2,1,0:T(8,128)S(1)} %get-tuple-element, ...), custom_call_target="tpu_custom_call" | custom-call | bytes 2600000 | tf_op jit(solution)/shard_map/pallas_call | solution.py:362
  13.8 0.9 %collective-permute-done.ux_ref = f32[2,16,128]{2,1,0:T(8,128)S(1)} collective-permute-done((f32[2,16,128]{2,1,0:T(8,128)S(1)}, f32[2,16,128]{2,1,0:T(8,128)S(1)}, u32[]{:S(2)}, u32[]{:S(2)}) %collective-permute-start) | collective-permute-done | bytes 16416 | tf_op jit(solution)/shard_map/ppermute | solution.py:324
  14.7 0.7 %shard_map.149 = (f32[3,8,16,128]{3,2,1,0:T(8,128)S(1)}, f32[2,16,128]{2,1,0:T(8,128)S(1)}, f32[2,8,128]{2,1,0:T(8,128)S(1)}, f32[2,24,128]{2,1,0:T(8,128)S(1)}) custom-call(f32[6]{0:T(128)S(1)} %convert_element_type.3.keep, f32[3,8,16,128]{3,2,1,0:T(8,128)S(1)} %get-tuple-element.47.part_ref, f32[2,16,128]{2,1,0:T(8,128)S(1)} %collective-permute-done.ux_ref, ...), custom_call_target="tpu_custom_call" | custom-call | bytes 500000 | tf_op jit(solution)/shard_map/pallas_call | solution.py:370
  15.4 0.3 collective-permute-start.5
  15.7 2.3 %collective-permute-start.3 = (f32[2,16,128]{2,1,0:T(8,128)S(1)}, f32[2,16,128]{2,1,0:T(8,128)S(1)}, u32[]{:S(2)}, u32[]{:S(2)}) collective-permute-start(f32[2,16,128]{2,1,0:T(8,128)S(1)} %get-tuple-element.52), channel_id=1, source_target_pairs={{0,16},{16,32},{32,48},{48,64},{64,80},{80,96},{96,112},{112,128},... | collective-permute-start | bytes 49160 | tf_op jit(solution)/shard_map/ppermute | solution.py:324
  18.1 0.5 shard_map.151
  18.6 0.2 shard_map.150
  18.8 3.0 %collective-permute-done.4.dy_ref = f32[2,8,128]{2,1,0:T(8,128)S(1)} collective-permute-done((f32[2,8,128]{2,1,0:T(8,128)S(1)}, f32[2,8,128]{2,1,0:T(8,128)S(1)}, u32[]{:S(2)}, u32[]{:S(2)}) %collective-permute-start.4) | collective-permute-done | bytes 8224 | tf_op jit(solution)/shard_map/ppermute | solution.py:324
  21.8 1.0 %shard_map.152 = (f32[3,8,16,128]{3,2,1,0:T(8,128)S(1)}, bf16[2,128,128]{2,1,0:T(8,128)(2,1)S(1)}) custom-call(f32[6]{0:T(128)S(1)} %convert_element_type.3.keep, f32[3,8,16,128]{3,2,1,0:T(8,128)S(1)} %get-tuple-element.51.h_ref, f32[2,16,128]{2,1,0:T(8,128)S(1)} %collective-permute-done.3.dx_ref, f32[2,8,128]{2,1,0:T(8,128)S(1)} %collective-permute-done.4.dy_ref, ...), custom_call_target="tpu_custom_call" | custom-call | bytes 1200000 | tf_op jit(solution)/shard_map/pallas_call | solution.py:385
  22.8 14.3 %all_to_all.21 = bf16[32,8,128]{2,1,0:T(8,128)(2,1)S(1)} all-to-all(bf16[32,8,128]{2,1,0:T(8,128)(2,1)S(1)} %bitcast.22), channel_id=1, replica_groups=mesh['gxc'=8,'core'=2,'gyh'=4,'gyl'=2,'gz'=2] {'gz','gxc','core'}, dimensions={0} | all-to-all | bytes 131072 | tf_op jit(solution)/shard_map/all_to_all | solution.py:392
  37.1 0.5 shard_map.154
  37.7 0.5 collective-permute-start.6
  38.2 1.4 %shard_map.155 = f32[8,3,8,16,128]{4,3,2,1,0:T(8,128)} custom-call(f32[1,8]{1,0:T(1,128)S(1)} %get-tuple-element.55.decay_ref, f32[1,8]{1,0:T(1,128)S(1)} %get-tuple-element.56.gain_ref, f32[8,3,8,16,128]{4,3,2,1,0:T(8,128)S(1)} %get-tuple-element.59.poles_ref, f32[3,8,16,128]{3,2,1,0:T(8,128)S(1)} %get-tuple-element.70.drive_ref), custom_call_target="tpu_custom_call" | custom-call | bytes 3400000 | tf_op jit(solution)/shard_map/pallas_call | solution.py:393
  39.6 0.4 shard_map.156
  40.0 9.3 %all_to_all.22.got_ref = f32[16,32,128]{2,1,0:T(8,128)S(1)} all-to-all(f32[16,32,128]{2,1,0:T(8,128)S(1)} %shard_map.156), channel_id=1, replica_groups=mesh['gxc'=8,'core'=2,'gyh'=4,'gyl'=2,'gz'=2] {'gxc','gyl'}, dimensions={0} | all-to-all | bytes 524288 | tf_op jit(solution)/shard_map/all_to_all | solution.py:413
  49.3 1.4 %collective-permute-start.7 = (f32[32,128]{1,0:T(8,128)S(1)}, f32[32,128]{1,0:T(8,128)S(1)}, u32[]{:S(2)}, u32[]{:S(2)}) collective-permute-start(f32[32,128]{1,0:T(8,128)S(1)} %shard_map.157.mine_ref), channel_id=1, source_target_pairs={{0,16},{16,0},{1,17},{17,1},{2,18},{18,2},{3,19},{19,3},{4,20},{20... | collective-permute-start | bytes 49160 | tf_op jit(solution)/shard_map/ppermute | solution.py:415
  50.8 0.8 %shard_map.153 = (f32[3,8,16,128]{3,2,1,0:T(8,128)}, f32[3,8,16,128]{3,2,1,0:T(8,128)}) custom-call(f32[3,8,16,128]{3,2,1,0:T(8,128)S(1)} %get-tuple-element.70.drive_ref, f32[3,8,16,128]{3,2,1,0:T(8,128)S(1)} %get-tuple-element.62.base_ref, f32[8,16,128]{2,1,0:T(8,128)S(1)} %get-tuple-element.63.slope_ref, f32[3,8,16,128]{3,2,1,0:T(8,128)S(1)} %get-tuple-element.51.h_ref), custom_call_target="tpu_custom_call" | custom-call | bytes 1200000 | tf_op jit(solution)/shard_map/pallas_call | solution.py:396
  51.6 0.2 shard_map.158
  51.9 15.0 %all_to_all.23 = f32[64,4,128]{2,1,0:T(4,128)S(1)} all-to-all(f32[64,4,128]{2,1,0:T(4,128)S(1)} %bitcast.21), channel_id=1, replica_groups=mesh['gxc'=8,'core'=2,'gyh'=4,'gyl'=2,'gz'=2] {'gyh','gyl','gxc'}, dimensions={0} | all-to-all | bytes 262144 | tf_op jit(solution)/shard_map/all_to_all | solution.py:420
  66.9 0.7 %shard_map.159 = f32[2,2,2048]{2,1,0:T(2,128)} custom-call(f32[256,128]{1,0:T(8,128)S(1)} %bitcast.19), custom_call_target="tpu_custom_call" | custom-call | bytes 300000 | tf_op jit(solution)/shard_map/pallas_call | solution.py:421
  (14 shorter events, 0.2 us)
Async XLA Ops:
  1.7 13.0 %collective-permute-start.1 = (f32[2,32,128]{2,1,0:T(8,128)S(1)}, f32[2,32,128]{2,1,0:T(8,128)S(1)}, u32[]{:S(2)}, u32[]{:S(2)}) collective-permute-start(f32[2,32,128]{2,1,0:T(8,128)S(1)} %get-tuple-element.49), channel_id=1, source_target_pairs={{0,14},{2,0},{4,2},{6,4},{8,6},{10,8},{12,10},{14,12},{1,15},{3,1}... | collective-permute-start | bytes 98312 | tf_op jit(solution)/shard_map/ppermute | solution.py:324
  8.2 6.5 %collective-permute-start.2 = (f32[2,24,128]{2,1,0:T(8,128)S(1)}, f32[2,24,128]{2,1,0:T(8,128)S(1)}, u32[]{:S(2)}, u32[]{:S(2)}) collective-permute-start(f32[2,24,128]{2,1,0:T(8,128)S(1)} %get-tuple-element.50), channel_id=1, source_target_pairs={{1,0},{0,129},{33,32},{32,161},{65,64},{64,193},{97,96},{96,225},{... | collective-permute-start | bytes 73736 | tf_op jit(solution)/shard_map/ppermute | solution.py:356
  10.9 3.8 %collective-permute-start = (f32[2,16,128]{2,1,0:T(8,128)S(1)}, f32[2,16,128]{2,1,0:T(8,128)S(1)}, u32[]{:S(2)}, u32[]{:S(2)}) collective-permute-start(f32[2,16,128]{2,1,0:T(8,128)S(1)} %get-tuple-element.48), channel_id=1, source_target_pairs={{0,240},{16,0},{32,16},{48,32},{64,48},{80,64},{96,80},{112,96},{1... | collective-permute-start | bytes 49160 | tf_op jit(solution)/shard_map/ppermute | solution.py:324
  15.4 21.7 %copy-start = (bf16[4,128,2048]{2,1,0:T(8,128)(2,1)S(1)}, bf16[4,128,2048]{2,1,0:T(8,128)(2,1)}, u32[]{:S(2)}) copy-start(bf16[4,128,2048]{2,1,0:T(8,128)(2,1)} %param.22) | copy-start | bytes 6291460
  15.4 6.4 %collective-permute-start.5 = (f32[2,24,128]{2,1,0:T(8,128)S(1)}, f32[2,24,128]{2,1,0:T(8,128)S(1)}, u32[]{:S(2)}, u32[]{:S(2)}) collective-permute-start(f32[2,24,128]{2,1,0:T(8,128)S(1)} %get-tuple-element.54), channel_id=1, source_target_pairs={{0,1},{1,128},{32,33},{33,160},{64,65},{65,192},{96,97},{97,224},{... | collective-permute-start | bytes 73736 | tf_op jit(solution)/shard_map/ppermute | solution.py:372
  15.7 6.1 %collective-permute-start.3 = (f32[2,16,128]{2,1,0:T(8,128)S(1)}, f32[2,16,128]{2,1,0:T(8,128)S(1)}, u32[]{:S(2)}, u32[]{:S(2)}) collective-permute-start(f32[2,16,128]{2,1,0:T(8,128)S(1)} %get-tuple-element.52), channel_id=1, source_target_pairs={{0,16},{16,32},{32,48},{48,64},{64,80},{80,96},{96,112},{112,128},... | collective-permute-start | bytes 49160 | tf_op jit(solution)/shard_map/ppermute | solution.py:324
  18.1 3.7 %collective-permute-start.4 = (f32[2,8,128]{2,1,0:T(8,128)S(1)}, f32[2,8,128]{2,1,0:T(8,128)S(1)}, u32[]{:S(2)}, u32[]{:S(2)}) collective-permute-start(f32[2,8,128]{2,1,0:T(8,128)S(1)} %get-tuple-element.53), channel_id=1, source_target_pairs={{0,2},{2,4},{4,6},{6,8},{8,10},{10,12},{12,14},{14,0},{1,3},{3,5},... | collective-permute-start | bytes 24584 | tf_op jit(solution)/shard_map/ppermute | solution.py:324
  37.7 1.9 %collective-permute-start.6 = (f32[16,32,128]{2,1,0:T(8,128)S(1)}, f32[16,32,128]{2,1,0:T(8,128)S(1)}, u32[]{:S(2)}, u32[]{:S(2)}) collective-permute-start(f32[16,32,128]{2,1,0:T(8,128)S(1)} %get-tuple-element.79), channel_id=1, source_target_pairs={{0,16},{16,0},{1,17},{17,1},{2,18},{18,2},{3,19},{19,3},{4,20},{20... | collective-permute-start | bytes 786440 | tf_op jit(solution)/shard_map/ppermute | solution.py:408
  39.6 12.0 %copy-start.1 = (bf16[2,256,192]{2,1,0:T(8,128)(2,1)S(1)}, bf16[2,256,192]{2,1,0:T(8,128)(2,1)}, u32[]{:S(2)}) copy-start(bf16[2,256,192]{2,1,0:T(8,128)(2,1)} %constant.33.clone.table_ref) | copy-start | bytes 589828
  49.3 2.3 %collective-permute-start.7 = (f32[32,128]{1,0:T(8,128)S(1)}, f32[32,128]{1,0:T(8,128)S(1)}, u32[]{:S(2)}, u32[]{:S(2)}) collective-permute-start(f32[32,128]{1,0:T(8,128)S(1)} %shard_map.157.mine_ref), channel_id=1, source_target_pairs={{0,16},{16,0},{1,17},{17,1},{2,18},{18,2},{3,19},{19,3},{4,20},{20... | collective-permute-start | bytes 49160 | tf_op jit(solution)/shard_map/ppermute | solution.py:415

commit v4 on v3

--- a/solution.py
+++ b/solution.py
@@ -100,29 +100,36 @@
         copy.wait()
 
 
-def mag_body(keep, part_ref, ux_ref, uy_ref, uz_ref, out_ref, gx_ref, gy_ref, gz_ref):
-    nx = part_ref.shape[1]
-    lane = lanes(16, 128)
-    row = rows(16, 128)
+def upper_terms(keep, ux_ref, uy_ref, uz_ref):
+    lane, row = lanes(16, 128), rows(16, 128)
     up_x = [ux_ref[part] * (0.5 * keep[0]) for part in range(2)]
     up_y = [uy_ref[part] * (0.5 * keep[1]) for part in range(2)]
     up_z = [uz_ref[part, 0:16, :] * (0.5 * keep[2]) for part in range(2)]
-    face_z = [jnp.zeros((16, 128), F32), jnp.zeros((16, 128), F32)]
-    gy_ref[...] = jnp.zeros_like(gy_ref)
-    for i in range(nx):
+
+    def whole(part_ref, i):
         ex_z, ey_z = [jnp.where(lane == 127, pltpu.roll(v, 127 - i, 1), 0.0) for v in up_z]
         ex_y, ez_y = [jnp.where(row == 15, v[i : i + 1], 0.0) for v in up_y]
         hx = part_ref[0, i] + (ey_z - ez_y)
         hy = part_ref[1, i] - ex_z
         hz = part_ref[2, i] + ex_y
-        if i == nx - 1:
+        if i == part_ref.shape[1] - 1:
             hy = hy + up_x[1]
             hz = hz - up_x[0]
+        return hx, hy, hz
+
+    return whole
+
+
+def edge_body(keep, part_ref, ux_ref, uy_ref, uz_ref, gx_ref, gy_ref, gz_ref):
+    nx = part_ref.shape[1]
+    lane = lanes(16, 128)
+    whole = upper_terms(keep, ux_ref, uy_ref, uz_ref)
+    face_z = [jnp.zeros((16, 128), F32), jnp.zeros((16, 128), F32)]
+    for i in range(nx):
+        hx, hy, hz = whole(part_ref, i)
+        if i == nx - 1:
             gx_ref[0] = hy
             gx_ref[1] = hz
-        out_ref[0, i] = hx
-        out_ref[1, i] = hy
-        out_ref[2, i] = hz
         gy_ref[0, i : i + 1, :] = hx[15:16]
         gy_ref[1, i : i + 1, :] = hz[15:16]
         for part, value in enumerate((hx, hy)):
@@ -130,6 +137,23 @@
     for part in range(2):
         gz_ref[part, 0:16, :] = face_z[part]
         gz_ref[part, 16:24, :] = jnp.zeros((8, 128), F32)
+
+
+def mag_body(keep, part_ref, ux_ref, uy_ref, uz_ref, out_ref, drive_ref):
+    lane, row = lanes(16, 128), rows(16, 128)
+    whole = upper_terms(keep, ux_ref, uy_ref, uz_ref)
+    hy_x = hz_x = jnp.zeros((16, 128), F32)
+    for i in range(part_ref.shape[1]):
+        hx, hy, hz = whole(part_ref, i)
+        out_ref[0, i] = hx
+        out_ref[1, i] = hy
+        out_ref[2, i] = hz
+        hx_y, hz_y = [jnp.where(row == 0, 0.0, pltpu.roll(v, 1, 0)) for v in (hx, hz)]
+        hx_z, hy_z = [jnp.where(lane == 0, 0.0, pltpu.roll(v, 1, 1)) for v in (hx, hy)]
+        drive_ref[0, i] = (hz - hz_y) - (hy - hy_z)
+        drive_ref[1, i] = (hx - hx_z) - (hz - hz_x)
+        drive_ref[2, i] = (hy - hy_x) - (hx - hx_y)
+        hy_x, hz_x = hy, hz
 
 
 def wall_body(decay_ref, gain_ref, poles_ref, e_ref, eps_ref, wall_ref, base_out, slope_out):
@@ -146,29 +170,27 @@
 
 
 def elec_body(
-    keep, h_ref, dx_ref, dy_ref, dz_ref, base_ref, slope_ref, select_ref, cell_ref, past_ref,
+    keep, part_ref, dx_ref, dy_ref, dz_ref, base_ref, slope_ref, select_ref, cell_ref, past_ref,
     drive_out, pack_out, cells,
 ):
-    nx = h_ref.shape[1]
+    nx = part_ref.shape[1]
     lane = lanes(16, 128)
     row = rows(16, 128)
     dn_x = [dx_ref[part] * keep[3] for part in range(2)]
     dn_y = [dy_ref[part] * keep[4] for part in range(2)]
     dn_z = [dz_ref[part, 0:16, :] * keep[5] for part in range(2)]
     for i in range(nx):
-        hx, hy, hz = h_ref[0, i], h_ref[1, i], h_ref[2, i]
-        hy_x = h_ref[1, i - 1] if i else dn_x[0]
-        hz_x = h_ref[2, i - 1] if i else dn_x[1]
-        hx_y = jnp.where(row == 0, dn_y[0][i : i + 1], pltpu.roll(hx, 1, 0))
-        hz_y = jnp.where(row == 0, dn_y[1][i : i + 1], pltpu.roll(hz, 1, 0))
         low = [v if i == 0 else pltpu.roll(v, 128 - i, 1) for v in dn_z]
-        hx_z = jnp.where(lane == 0, low[0], pltpu.roll(hx, 1, 1))
-        hy_z = jnp.where(lane == 0, low[1], pltpu.roll(hy, 1, 1))
+        hx_z, hy_z = [jnp.where(lane == 0, v, 0.0) for v in low]
+        hx_y, hz_y = [jnp.where(row == 0, v[i : i + 1], 0.0) for v in dn_y]
         drive = [
-            (hz - hz_y) - (hy - hy_z),
-            (hx - hx_z) - (hz - hz_x),
-            (hy - hy_x) - (hx - hx_y),
+            part_ref[0, i] + (hy_z - hz_y),
+            part_ref[1, i] - hx_z,
+            part_ref[2, i] + hx_y,
         ]
+        if i == 0:
+            drive[1] = drive[1] + dn_x[1]
+            drive[2] = drive[2] - dn_x[0]
         for comp in range(3):
             drive_out[comp, i] = drive[comp]
         span = pl.ds(i * 16, 16)
@@ -367,10 +389,11 @@
         data=2600000,
     )(e_near, h_near, *[far_off(value) for value in later])
 
-    h_mid, *far = call(mag_body, [block, *faces_up], [SM] + [VM] * 4, data=500000)(keep, inner, *up)
+    far = call(edge_body, faces_up, [SM] + [VM] * 4, data=500000)(keep, inner, *up)
     down = [shift(face, axis, 1) for face, axis in zip(far[:2], axes)]
     down.append(lax.ppermute(far[2], ("gxc", "gz"), cross(0)))
-    far, owners, poles = lax.optimization_barrier((far, owners, poles))
+    far, owners, poles, inner = lax.optimization_barrier((far, owners, poles, inner))
+    h_mid, part = call(mag_body, [block, block], [SM] + [VM] * 4, data=500000)(keep, inner, *up)
     select, cell, leaving = call(
         pack_body,
         [struct(2, 128, 32), struct(2, 32, 128), struct(128, 128)],
@@ -388,7 +411,7 @@
         [SM] + [VM] * 9,
         scratch=[pltpu.VMEM((2, 128, 128), BF16)],
         data=1200000,
-    )(keep, h_mid, *down, base, slope, select, cell, leaving)
+    )(keep, part, *down, base, slope, select, cell, leaving)
     arrived = lax.all_to_all(leaving.reshape(32, 8, 128), ("gz", *GX), 0, 0, tiled=True)
     poles_next = call(poles_body, struct(*poles.shape), [VM] * 4, data=3400000)(
         decay, gain, poles, drive

time: 67.8 us -> 67.8 us (level)
  waiting for transfers between devices: 3.96 us -> 3.22 us
  Pallas kernels: 9.12 us -> 9.8 us
    ppermute x4, waiting for transfers between devices: 3.9 us -> 3.16 us  [shift(): lax.ppermute(value, axis, [(i, (i + step) % count) for i in range(count)])]
    pallas_call x1 -> x2, Pallas kernels: 0.73 us -> 1.46 us  [the longest x1 0.73 us: per_device(): call(mag_body, [block, block], [SM] + [VM] * 4, data=500000)]
  transfers between devices with their start and end apart: 8 -> 8, of which waited for: 3 -> 3; matrix products, arithmetic and copies ran while one was open for 0% -> 0% of each run, Pallas kernels for 7% -> 8%
where the time goes in v4:
time: 67.8 us; the launch traced here: 67.5 us
  blocking collectives  38.6 us (57%)
  starting transfers between devices  15 us (22%)
  Pallas kernels  9.8 us (14%)
  waiting for transfers between devices  3.22 us (5%)
  between operations  0.73 us (1%)
    all_to_all x1, blocking collectives, per_device(): spectra = lax.all_to_all(spectra, (*GY, 'gxc'), 0, 0, tiled=True)  15 us
    all_to_all x1, blocking collectives, per_device(): lax.all_to_all(leaving.reshape(32, 8, 128), ('gz', *GX), 0, 0, tiled=True)  14.3 us
    ppermute x4, starting transfers between devices, shift(): lax.ppermute(value, axis, [(i, (i + step) % count) for i in range(count)])  10.1 us
    all_to_all x1, blocking collectives, per_device(): part = lax.all_to_all(part, ('gxc', 'gyl'), 0, 0, tiled=True)  9.31 us
    ppermute x4, waiting for transfers between devices, shift(): lax.ppermute(value, axis, [(i, (i + step) % count) for i in range(count)])  3.16 us
    ppermute x1, starting transfers between devices, per_device(): up.append(lax.ppermute(near[2], ('gxc', 'gz'), cross(1)))  2.73 us
    pallas_call x1, Pallas kernels, per_device(): call(inner_body, [block, *[struct(*value.shape, dtype=value.dtype) for va...  1.49 us
    pallas_call x1, Pallas kernels, per_device(): call(poles_body, struct(*poles.shape), [VM] * 4, data=3400000)  1.44 us
  transfers between devices with their start and end apart: 8, of which 3 were waited for; matrix products, arithmetic and copies ran while one was open for 0% of the time, Pallas kernels for 8%

profile of v4, /device:TPU:1, one launch (start us, length us, event | category | flops | bytes accessed | tf_op | source)
XLA Modules:
  0.0 67.5 jit_solution(833007664040602218)
XLA Ops:
  0.6 1.1 %shard_map.147 = (f32[2,16,128]{2,1,0:T(8,128)S(1)}, f32[2,32,128]{2,1,0:T(8,128)S(1)}, f32[2,24,128]{2,1,0:T(8,128)S(1)}, f32[3,8,16,128]{3,2,1,0:T(8,128)S(1)}, f32[3,8,16,128]{3,2,1,0:T(8,128)S(1)}) custom-call(f32[3,8,16,128]{3,2,1,0:T(8,128)} %e_far.1, f32[3,8,16,128]{3,2,1,0:T(8,128)} %h_far.1), custom_call_target="tpu_custom_call" | custom-call | bytes 400000 | tf_op jit(solution)/shard_map/pallas_call | solution.py:374
  1.7 6.5 %collective-permute-start.1 = (f32[2,32,128]{2,1,0:T(8,128)S(1)}, f32[2,32,128]{2,1,0:T(8,128)S(1)}, u32[]{:S(2)}, u32[]{:S(2)}) collective-permute-start(f32[2,32,128]{2,1,0:T(8,128)S(1)} %get-tuple-element.51), channel_id=1, source_target_pairs={{0,14},{2,0},{4,2},{6,4},{8,6},{10,8},{12,10},{14,12},{1,15},{3,1}... | collective-permute-start | bytes 98312 | tf_op jit(solution)/shard_map/ppermute | solution.py:346
  8.2 2.7 %collective-permute-start.2 = (f32[2,24,128]{2,1,0:T(8,128)S(1)}, f32[2,24,128]{2,1,0:T(8,128)S(1)}, u32[]{:S(2)}, u32[]{:S(2)}) collective-permute-start(f32[2,24,128]{2,1,0:T(8,128)S(1)} %get-tuple-element.52), channel_id=1, source_target_pairs={{1,0},{0,129},{33,32},{32,161},{65,64},{64,193},{97,96},{96,225},{... | collective-permute-start | bytes 73736 | tf_op jit(solution)/shard_map/ppermute | solution.py:378
  10.9 1.2 %collective-permute-start = (f32[2,16,128]{2,1,0:T(8,128)S(1)}, f32[2,16,128]{2,1,0:T(8,128)S(1)}, u32[]{:S(2)}, u32[]{:S(2)}) collective-permute-start(f32[2,16,128]{2,1,0:T(8,128)S(1)} %get-tuple-element.50), channel_id=1, source_target_pairs={{0,240},{16,0},{32,16},{48,32},{64,48},{80,64},{96,80},{112,96},{1... | collective-permute-start | bytes 49160 | tf_op jit(solution)/shard_map/ppermute | solution.py:346
  12.3 1.5 %shard_map.148 = (f32[3,8,16,128]{3,2,1,0:T(8,128)S(1)}, f32[8,3,8,16,128]{4,3,2,1,0:T(8,128)S(1)}, f32[8,16,128]{2,1,0:T(8,128)S(1)}, s32[8,16,128]{2,1,0:T(8,1...) custom-call(f32[3,8,16,128]{3,2,1,0:T(8,128)S(1)} %get-tuple-element, ...), custom_call_target="tpu_custom_call" | custom-call | bytes 2600000 | tf_op jit(solution)/shard_map/pallas_call | solution.py:384
  13.8 0.9 %collective-permute-done.ux_ref = f32[2,16,128]{2,1,0:T(8,128)S(1)} collective-permute-done((f32[2,16,128]{2,1,0:T(8,128)S(1)}, f32[2,16,128]{2,1,0:T(8,128)S(1)}, u32[]{:S(2)}, u32[]{:S(2)}) %collective-permute-start) | collective-permute-done | bytes 16416 | tf_op jit(solution)/shard_map/ppermute | solution.py:346
  14.7 0.7 %shard_map.149 = (f32[2,16,128]{2,1,0:T(8,128)S(1)}, f32[2,8,128]{2,1,0:T(8,128)S(1)}, f32[2,24,128]{2,1,0:T(8,128)S(1)}) custom-call(f32[6]{0:T(128)S(1)} %convert_element_type.3.keep, f32[3,8,16,128]{3,2,1,0:T(8,128)S(1)} %get-tuple-element.58.part_ref, f32[2,16,128]{2,1,0:T(8,128)S(1)} %collective-permute-done.ux_ref, ...), custom_call_target="tpu_custom_call" | custom-call | bytes 500000 | tf_op jit(solution)/shard_map/pallas_call | solution.py:392
  15.4 0.3 collective-permute-start.5
  15.7 2.3 %collective-permute-start.3 = (f32[2,16,128]{2,1,0:T(8,128)S(1)}, f32[2,16,128]{2,1,0:T(8,128)S(1)}, u32[]{:S(2)}, u32[]{:S(2)}) collective-permute-start(f32[2,16,128]{2,1,0:T(8,128)S(1)} %get-tuple-element.53), channel_id=1, source_target_pairs={{0,16},{16,32},{32,48},{48,64},{64,80},{80,96},{96,112},{112,128},... | collective-permute-start | bytes 49160 | tf_op jit(solution)/shard_map/ppermute | solution.py:346
  18.1 0.7 %shard_map.150 = (f32[3,8,16,128]{3,2,1,0:T(8,128)S(1)}, f32[3,8,16,128]{3,2,1,0:T(8,128)S(1)}) custom-call(f32[6]{0:T(128)S(1)} %convert_element_type.3.keep, f32[3,8,16,128]{3,2,1,0:T(8,128)S(1)} %get-tuple-element.58.part_ref, f32[2,16,128]{2,1,0:T(8,128)S(1)} %collective-permute-done.ux_ref, f32[2,32,128]{2,1,0:T(8,128)S(1)} %collective-permute-done.1.uy_ref, ...), custom_call_target="tpu_custom_call" | custom-call | bytes 500000 | tf_op jit(solution)/shard_map/pallas_call | solution.py:396
  18.8 0.5 shard_map.152
  19.5 2.2 %collective-permute-done.4.dy_ref = f32[2,8,128]{2,1,0:T(8,128)S(1)} collective-permute-done((f32[2,8,128]{2,1,0:T(8,128)S(1)}, f32[2,8,128]{2,1,0:T(8,128)S(1)}, u32[]{:S(2)}, u32[]{:S(2)}) %collective-permute-start.4) | collective-permute-done | bytes 8224 | tf_op jit(solution)/shard_map/ppermute | solution.py:346
  21.8 1.0 %shard_map.153 = (f32[3,8,16,128]{3,2,1,0:T(8,128)S(1)}, bf16[2,128,128]{2,1,0:T(8,128)(2,1)S(1)}) custom-call(f32[6]{0:T(128)S(1)} %convert_element_type.3.keep, f32[3,8,16,128]{3,2,1,0:T(8,128)S(1)} %get-tuple-element.59.part_ref, f32[2,16,128]{2,1,0:T(8,128)S(1)} %collective-permute-done.3.dx_ref, f32[2,8,128]{2,1,0:T(8,128)S(1)} %collective-permute-done.4.dy_ref, ...), custom_call_target="tpu_custom_call" | custom-call | bytes 1200000 | tf_op jit(solution)/shard_map/pallas_call | solution.py:408
  22.8 14.3 %all_to_all.21 = bf16[32,8,128]{2,1,0:T(8,128)(2,1)S(1)} all-to-all(bf16[32,8,128]{2,1,0:T(8,128)(2,1)S(1)} %bitcast.22), channel_id=1, replica_groups=mesh['gxc'=8,'core'=2,'gyh'=4,'gyl'=2,'gz'=2] {'gz','gxc','core'}, dimensions={0} | all-to-all | bytes 131072 | tf_op jit(solution)/shard_map/all_to_all | solution.py:415
  37.1 0.5 shard_map.155
  37.6 0.5 collective-permute-start.6
  38.1 1.4 %shard_map.156 = f32[8,3,8,16,128]{4,3,2,1,0:T(8,128)} custom-call(f32[1,8]{1,0:T(1,128)S(1)} %get-tuple-element.60.decay_ref, f32[1,8]{1,0:T(1,128)S(1)} %get-tuple-element.61.gain_ref, f32[8,3,8,16,128]{4,3,2,1,0:T(8,128)S(1)} %get-tuple-element.62.poles_ref, f32[3,8,16,128]{3,2,1,0:T(8,128)S(1)} %get-tuple-element.74.drive_ref), custom_call_target="tpu_custom_call" | custom-call | bytes 3400000 | tf_op jit(solution)/shard_map/pallas_call | solution.py:416
  39.6 0.4 shard_map.157
  40.0 9.3 %all_to_all.22.got_ref = f32[16,32,128]{2,1,0:T(8,128)S(1)} all-to-all(f32[16,32,128]{2,1,0:T(8,128)S(1)} %shard_map.157), channel_id=1, replica_groups=mesh['gxc'=8,'core'=2,'gyh'=4,'gyl'=2,'gz'=2] {'gxc','gyl'}, dimensions={0} | all-to-all | bytes 524288 | tf_op jit(solution)/shard_map/all_to_all | solution.py:436
  49.3 1.4 %collective-permute-start.7 = (f32[32,128]{1,0:T(8,128)S(1)}, f32[32,128]{1,0:T(8,128)S(1)}, u32[]{:S(2)}, u32[]{:S(2)}) collective-permute-start(f32[32,128]{1,0:T(8,128)S(1)} %shard_map.158.mine_ref), channel_id=1, source_target_pairs={{0,16},{16,0},{1,17},{17,1},{2,18},{18,2},{3,19},{19,3},{4,20},{20... | collective-permute-start | bytes 49160 | tf_op jit(solution)/shard_map/ppermute | solution.py:438
  50.7 0.8 %shard_map.154 = (f32[3,8,16,128]{3,2,1,0:T(8,128)}, f32[3,8,16,128]{3,2,1,0:T(8,128)}) custom-call(f32[3,8,16,128]{3,2,1,0:T(8,128)S(1)} %get-tuple-element.74.drive_ref, f32[3,8,16,128]{3,2,1,0:T(8,128)S(1)} %get-tuple-element.65.base_ref, f32[8,16,128]{2,1,0:T(8,128)S(1)} %get-tuple-element.66.slope_ref, f32[3,8,16,128]{3,2,1,0:T(8,128)S(1)} %get-tuple-element.70.h_ref), custom_call_target="tpu_custom_call" | custom-call | bytes 1200000 | tf_op jit(solution)/shard_map/pallas_call | solution.py:419
  51.5 0.2 shard_map.159
  51.8 15.0 %all_to_all.23 = f32[64,4,128]{2,1,0:T(4,128)S(1)} all-to-all(f32[64,4,128]{2,1,0:T(4,128)S(1)} %bitcast.21), channel_id=1, replica_groups=mesh['gxc'=8,'core'=2,'gyh'=4,'gyl'=2,'gz'=2] {'gyh','gyl','gxc'}, dimensions={0} | all-to-all | bytes 262144 | tf_op jit(solution)/shard_map/all_to_all | solution.py:443
  66.8 0.7 %shard_map.160 = f32[2,2,2048]{2,1,0:T(2,128)} custom-call(f32[256,128]{1,0:T(8,128)S(1)} %bitcast.19), custom_call_target="tpu_custom_call" | custom-call | bytes 300000 | tf_op jit(solution)/shard_map/pallas_call | solution.py:444
  (15 shorter events, 0.4 us)
Async XLA Ops:
  1.7 13.0 %collective-permute-start.1 = (f32[2,32,128]{2,1,0:T(8,128)S(1)}, f32[2,32,128]{2,1,0:T(8,128)S(1)}, u32[]{:S(2)}, u32[]{:S(2)}) collective-permute-start(f32[2,32,128]{2,1,0:T(8,128)S(1)} %get-tuple-element.51), channel_id=1, source_target_pairs={{0,14},{2,0},{4,2},{6,4},{8,6},{10,8},{12,10},{14,12},{1,15},{3,1}... | collective-permute-start | bytes 98312 | tf_op jit(solution)/shard_map/ppermute | solution.py:346
  8.2 6.5 %collective-permute-start.2 = (f32[2,24,128]{2,1,0:T(8,128)S(1)}, f32[2,24,128]{2,1,0:T(8,128)S(1)}, u32[]{:S(2)}, u32[]{:S(2)}) collective-permute-start(f32[2,24,128]{2,1,0:T(8,128)S(1)} %get-tuple-element.52), channel_id=1, source_target_pairs={{1,0},{0,129},{33,32},{32,161},{65,64},{64,193},{97,96},{96,225},{... | collective-permute-start | bytes 73736 | tf_op jit(solution)/shard_map/ppermute | solution.py:378
  10.9 3.8 %collective-permute-start = (f32[2,16,128]{2,1,0:T(8,128)S(1)}, f32[2,16,128]{2,1,0:T(8,128)S(1)}, u32[]{:S(2)}, u32[]{:S(2)}) collective-permute-start(f32[2,16,128]{2,1,0:T(8,128)S(1)} %get-tuple-element.50), channel_id=1, source_target_pairs={{0,240},{16,0},{32,16},{48,32},{64,48},{80,64},{96,80},{112,96},{1... | collective-permute-start | bytes 49160 | tf_op jit(solution)/shard_map/ppermute | solution.py:346
  15.4 6.4 %collective-permute-start.5 = (f32[2,24,128]{2,1,0:T(8,128)S(1)}, f32[2,24,128]{2,1,0:T(8,128)S(1)}, u32[]{:S(2)}, u32[]{:S(2)}) collective-permute-start(f32[2,24,128]{2,1,0:T(8,128)S(1)} %get-tuple-element.55), channel_id=1, source_target_pairs={{0,1},{1,128},{32,33},{33,160},{64,65},{65,192},{96,97},{97,224},{... | collective-permute-start | bytes 73736 | tf_op jit(solution)/shard_map/ppermute | solution.py:394
  15.7 6.1 %collective-permute-start.3 = (f32[2,16,128]{2,1,0:T(8,128)S(1)}, f32[2,16,128]{2,1,0:T(8,128)S(1)}, u32[]{:S(2)}, u32[]{:S(2)}) collective-permute-start(f32[2,16,128]{2,1,0:T(8,128)S(1)} %get-tuple-element.53), channel_id=1, source_target_pairs={{0,16},{16,32},{32,48},{48,64},{64,80},{80,96},{96,112},{112,128},... | collective-permute-start | bytes 49160 | tf_op jit(solution)/shard_map/ppermute | solution.py:346
  18.1 3.7 %collective-permute-start.4 = (f32[2,8,128]{2,1,0:T(8,128)S(1)}, f32[2,8,128]{2,1,0:T(8,128)S(1)}, u32[]{:S(2)}, u32[]{:S(2)}) collective-permute-start(f32[2,8,128]{2,1,0:T(8,128)S(1)} %get-tuple-element.54), channel_id=1, source_target_pairs={{0,2},{2,4},{4,6},{6,8},{8,10},{10,12},{12,14},{14,0},{1,3},{3,5},... | collective-permute-start | bytes 24584 | tf_op jit(solution)/shard_map/ppermute | solution.py:346
  18.8 18.3 %copy-start = (bf16[4,128,2048]{2,1,0:T(8,128)(2,1)S(1)}, bf16[4,128,2048]{2,1,0:T(8,128)(2,1)}, u32[]{:S(2)}) copy-start(bf16[4,128,2048]{2,1,0:T(8,128)(2,1)} %param.22) | copy-start | bytes 6291460
  37.6 1.9 %collective-permute-start.6 = (f32[16,32,128]{2,1,0:T(8,128)S(1)}, f32[16,32,128]{2,1,0:T(8,128)S(1)}, u32[]{:S(2)}, u32[]{:S(2)}) collective-permute-start(f32[16,32,128]{2,1,0:T(8,128)S(1)} %get-tuple-element.83), channel_id=1, source_target_pairs={{0,16},{16,0},{1,17},{17,1},{2,18},{18,2},{3,19},{19,3},{4,20},{20... | collective-permute-start | bytes 786440 | tf_op jit(solution)/shard_map/ppermute | solution.py:431
  39.6 12.0 %copy-start.1 = (bf16[2,256,192]{2,1,0:T(8,128)(2,1)S(1)}, bf16[2,256,192]{2,1,0:T(8,128)(2,1)}, u32[]{:S(2)}) copy-start(bf16[2,256,192]{2,1,0:T(8,128)(2,1)} %constant.33.clone.table_ref) | copy-start | bytes 589828
  49.3 2.2 %collective-permute-start.7 = (f32[32,128]{1,0:T(8,128)S(1)}, f32[32,128]{1,0:T(8,128)S(1)}, u32[]{:S(2)}, u32[]{:S(2)}) collective-permute-start(f32[32,128]{1,0:T(8,128)S(1)} %shard_map.158.mine_ref), channel_id=1, source_target_pairs={{0,16},{16,0},{1,17},{17,1},{2,18},{18,2},{3,19},{19,3},{4,20},{20... | collective-permute-start | bytes 49160 | tf_op jit(solution)/shard_map/ppermute | solution.py:438

commit v5 on v4

--- a/solution.py
+++ b/solution.py
@@ -100,11 +100,11 @@
         copy.wait()
 
 
-def upper_terms(keep, ux_ref, uy_ref, uz_ref):
+def upper_terms(keep_ref, ux_ref, uy_ref, uz_ref):
     lane, row = lanes(16, 128), rows(16, 128)
-    up_x = [ux_ref[part] * (0.5 * keep[0]) for part in range(2)]
-    up_y = [uy_ref[part] * (0.5 * keep[1]) for part in range(2)]
-    up_z = [uz_ref[part, 0:16, :] * (0.5 * keep[2]) for part in range(2)]
+    up_x = [ux_ref[part] * (0.5 * keep_ref[0 : 0 + 1, :]) for part in range(2)]
+    up_y = [uy_ref[part] * (0.5 * keep_ref[1 : 1 + 1, :]) for part in range(2)]
+    up_z = [uz_ref[part, 0:16, :] * (0.5 * keep_ref[2 : 2 + 1, :]) for part in range(2)]
 
     def whole(part_ref, i):
         ex_z, ey_z = [jnp.where(lane == 127, pltpu.roll(v, 127 - i, 1), 0.0) for v in up_z]
@@ -120,10 +120,10 @@
     return whole
 
 
-def edge_body(keep, part_ref, ux_ref, uy_ref, uz_ref, gx_ref, gy_ref, gz_ref):
+def edge_body(keep_ref, part_ref, ux_ref, uy_ref, uz_ref, gx_ref, gy_ref, gz_ref):
     nx = part_ref.shape[1]
     lane = lanes(16, 128)
-    whole = upper_terms(keep, ux_ref, uy_ref, uz_ref)
+    whole = upper_terms(keep_ref, ux_ref, uy_ref, uz_ref)
     face_z = [jnp.zeros((16, 128), F32), jnp.zeros((16, 128), F32)]
     for i in range(nx):
         hx, hy, hz = whole(part_ref, i)
@@ -139,9 +139,9 @@
         gz_ref[part, 16:24, :] = jnp.zeros((8, 128), F32)
 
 
-def mag_body(keep, part_ref, ux_ref, uy_ref, uz_ref, out_ref, drive_ref):
+def mag_body(keep_ref, part_ref, ux_ref, uy_ref, uz_ref, out_ref, drive_ref):
     lane, row = lanes(16, 128), rows(16, 128)
-    whole = upper_terms(keep, ux_ref, uy_ref, uz_ref)
+    whole = upper_terms(keep_ref, ux_ref, uy_ref, uz_ref)
     hy_x = hz_x = jnp.zeros((16, 128), F32)
     for i in range(part_ref.shape[1]):
         hx, hy, hz = whole(part_ref, i)
@@ -170,15 +170,15 @@
 
 
 def elec_body(
-    keep, part_ref, dx_ref, dy_ref, dz_ref, base_ref, slope_ref, select_ref, cell_ref, past_ref,
+    keep_ref, part_ref, dx_ref, dy_ref, dz_ref, base_ref, slope_ref, select_ref, cell_ref, past_ref,
     drive_out, pack_out, cells,
 ):
     nx = part_ref.shape[1]
     lane = lanes(16, 128)
     row = rows(16, 128)
-    dn_x = [dx_ref[part] * keep[3] for part in range(2)]
-    dn_y = [dy_ref[part] * keep[4] for part in range(2)]
-    dn_z = [dz_ref[part, 0:16, :] * keep[5] for part in range(2)]
+    dn_x = [dx_ref[part] * keep_ref[3 : 3 + 1, :] for part in range(2)]
+    dn_y = [dy_ref[part] * keep_ref[4 : 4 + 1, :] for part in range(2)]
+    dn_z = [dz_ref[part, 0:16, :] * keep_ref[5 : 5 + 1, :] for part in range(2)]
     for i in range(nx):
         low = [v if i == 0 else pltpu.roll(v, 128 - i, 1) for v in dn_z]
         hx_z, hy_z = [jnp.where(lane == 0, v, 0.0) for v in low]
@@ -366,6 +366,7 @@
         [(at < lax.axis_size(axis) - 1) for at, axis in zip(places, axes)]
         + [at > 0 for at in places]
     ).astype(F32)
+    keep = jnp.broadcast_to(keep[:, None], (6, 128))
     core = lax.axis_index("core").reshape(1)
     block = struct(3, nx, ny, nz)
     faces = [struct(2, ny, nz), struct(2, 4 * nx, nz), struct(2, ny + 8, 128)]
@@ -389,11 +390,11 @@
         data=2600000,
     )(e_near, h_near, *[far_off(value) for value in later])
 
-    far = call(edge_body, faces_up, [SM] + [VM] * 4, data=500000)(keep, inner, *up)
+    far = call(edge_body, faces_up, [VM] * 5, data=500000)(keep, inner, *up)
     down = [shift(face, axis, 1) for face, axis in zip(far[:2], axes)]
     down.append(lax.ppermute(far[2], ("gxc", "gz"), cross(0)))
     far, owners, poles, inner = lax.optimization_barrier((far, owners, poles, inner))
-    h_mid, part = call(mag_body, [block, block], [SM] + [VM] * 4, data=500000)(keep, inner, *up)
+    h_mid, part = call(mag_body, [block, block], [VM] * 5, data=500000)(keep, inner, *up)
     select, cell, leaving = call(
         pack_body,
         [struct(2, 128, 32), struct(2, 32, 128), struct(128, 128)],
@@ -408,7 +409,7 @@
     drive, leaving = call(
         elec_body,
         [block, struct(2, 128, 128, dtype=BF16)],
-        [SM] + [VM] * 9,
+        [VM] * 10,
         scratch=[pltpu.VMEM((2, 128, 128), BF16)],
         data=1200000,
     )(keep, part, *down, base, slope, select, cell, leaving)

time: 67.8 us -> 66.7 us (0.984)
  Pallas kernels: 9.8 us -> 8.18 us
    pallas_call x3, Pallas kernels: 2.44 us -> 0.82 us  [the longest x1 0.44 us: per_device(): call(elec_body, [block, struct(2, 128, 128, dtype=BF16)], [VM] * 10, scra...]
  transfers between devices with their start and end apart: 8 -> 8, of which waited for: 3 -> 3; matrix products, arithmetic and copies ran while one was open for 0% -> 0% of each run, Pallas kernels for 8% -> 7%
where the time goes in v5:
time: 66.7 us; the launch traced here: 66.5 us
  blocking collectives  38.6 us (58%)
  starting transfers between devices  15 us (22%)
  Pallas kernels  8.18 us (12%)
  waiting for transfers between devices  3.76 us (6%)
  between operations  0.73 us (1%)
    all_to_all x1, blocking collectives, per_device(): spectra = lax.all_to_all(spectra, (*GY, 'gxc'), 0, 0, tiled=True)  15 us
    all_to_all x1, blocking collectives, per_device(): lax.all_to_all(leaving.reshape(32, 8, 128), ('gz', *GX), 0, 0, tiled=True)  14.3 us
    ppermute x4, starting transfers between devices, shift(): lax.ppermute(value, axis, [(i, (i + step) % count) for i in range(count)])  10.1 us
    all_to_all x1, blocking collectives, per_device(): part = lax.all_to_all(part, ('gxc', 'gyl'), 0, 0, tiled=True)  9.31 us
    ppermute x4, waiting for transfers between devices, shift(): lax.ppermute(value, axis, [(i, (i + step) % count) for i in range(count)])  3.69 us
    ppermute x1, starting transfers between devices, per_device(): up.append(lax.ppermute(near[2], ('gxc', 'gz'), cross(1)))  2.73 us
    pallas_call x1, Pallas kernels, per_device(): call(inner_body, [block, *[struct(*value.shape, dtype=value.dtype) for va...  1.49 us
    pallas_call x1, Pallas kernels, per_device(): call(poles_body, struct(*poles.shape), [VM] * 4, data=3400000)  1.44 us
  transfers between devices with their start and end apart: 8, of which 3 were waited for; matrix products, arithmetic and copies ran while one was open for 0% of the time, Pallas kernels for 7%

profile of v5, /device:TPU:1, one launch (start us, length us, event | category | flops | bytes accessed | tf_op | source)
XLA Modules:
  0.0 66.5 jit_solution(2761811389932186658)
XLA Ops:
  0.6 1.1 %shard_map.147 = (f32[2,16,128]{2,1,0:T(8,128)S(1)}, f32[2,32,128]{2,1,0:T(8,128)S(1)}, f32[2,24,128]{2,1,0:T(8,128)S(1)}, f32[3,8,16,128]{3,2,1,0:T(8,128)S(1)}, f32[3,8,16,128]{3,2,1,0:T(8,128)S(1)}) custom-call(f32[3,8,16,128]{3,2,1,0:T(8,128)} %e_far.1, f32[3,8,16,128]{3,2,1,0:T(8,128)} %h_far.1), custom_call_target="tpu_custom_call" | custom-call | bytes 400000 | tf_op jit(solution)/shard_map/pallas_call | solution.py:375
  1.7 6.5 %collective-permute-start.1 = (f32[2,32,128]{2,1,0:T(8,128)S(1)}, f32[2,32,128]{2,1,0:T(8,128)S(1)}, u32[]{:S(2)}, u32[]{:S(2)}) collective-permute-start(f32[2,32,128]{2,1,0:T(8,128)S(1)} %get-tuple-element.51), channel_id=1, source_target_pairs={{0,14},{2,0},{4,2},{6,4},{8,6},{10,8},{12,10},{14,12},{1,15},{3,1}... | collective-permute-start | bytes 98312 | tf_op jit(solution)/shard_map/ppermute | solution.py:346
  8.2 2.7 %collective-permute-start.2 = (f32[2,24,128]{2,1,0:T(8,128)S(1)}, f32[2,24,128]{2,1,0:T(8,128)S(1)}, u32[]{:S(2)}, u32[]{:S(2)}) collective-permute-start(f32[2,24,128]{2,1,0:T(8,128)S(1)} %get-tuple-element.52), channel_id=1, source_target_pairs={{1,0},{0,129},{33,32},{32,161},{65,64},{64,193},{97,96},{96,225},{... | collective-permute-start | bytes 73736 | tf_op jit(solution)/shard_map/ppermute | solution.py:379
  10.9 1.2 %collective-permute-start = (f32[2,16,128]{2,1,0:T(8,128)S(1)}, f32[2,16,128]{2,1,0:T(8,128)S(1)}, u32[]{:S(2)}, u32[]{:S(2)}) collective-permute-start(f32[2,16,128]{2,1,0:T(8,128)S(1)} %get-tuple-element.50), channel_id=1, source_target_pairs={{0,240},{16,0},{32,16},{48,32},{64,48},{80,64},{96,80},{112,96},{1... | collective-permute-start | bytes 49160 | tf_op jit(solution)/shard_map/ppermute | solution.py:346
  12.3 1.5 %shard_map.148 = (f32[3,8,16,128]{3,2,1,0:T(8,128)S(1)}, f32[8,3,8,16,128]{4,3,2,1,0:T(8,128)S(1)}, f32[8,16,128]{2,1,0:T(8,128)S(1)}, s32[8,16,128]{2,1,0:T(8,1...) custom-call(f32[3,8,16,128]{3,2,1,0:T(8,128)S(1)} %get-tuple-element, ...), custom_call_target="tpu_custom_call" | custom-call | bytes 2600000 | tf_op jit(solution)/shard_map/pallas_call | solution.py:385
  13.8 0.9 %collective-permute-done.ux_ref = f32[2,16,128]{2,1,0:T(8,128)S(1)} collective-permute-done((f32[2,16,128]{2,1,0:T(8,128)S(1)}, f32[2,16,128]{2,1,0:T(8,128)S(1)}, u32[]{:S(2)}, u32[]{:S(2)}) %collective-permute-start) | collective-permute-done | bytes 16416 | tf_op jit(solution)/shard_map/ppermute | solution.py:346
  14.9 0.3 collective-permute-start.5
  15.2 2.3 %collective-permute-start.3 = (f32[2,16,128]{2,1,0:T(8,128)S(1)}, f32[2,16,128]{2,1,0:T(8,128)S(1)}, u32[]{:S(2)}, u32[]{:S(2)}) collective-permute-start(f32[2,16,128]{2,1,0:T(8,128)S(1)} %get-tuple-element.53), channel_id=1, source_target_pairs={{0,16},{16,32},{32,48},{48,64},{64,80},{80,96},{96,112},{112,128},... | collective-permute-start | bytes 49160 | tf_op jit(solution)/shard_map/ppermute | solution.py:346
  17.6 0.2 shard_map.150
  17.8 0.5 shard_map.152
  18.3 0.2 shard_map.151
  18.5 2.8 %collective-permute-done.4.dy_ref = f32[2,8,128]{2,1,0:T(8,128)S(1)} collective-permute-done((f32[2,8,128]{2,1,0:T(8,128)S(1)}, f32[2,8,128]{2,1,0:T(8,128)S(1)}, u32[]{:S(2)}, u32[]{:S(2)}) %collective-permute-start.4) | collective-permute-done | bytes 8224 | tf_op jit(solution)/shard_map/ppermute | solution.py:346
  21.3 0.4 shard_map.153
  21.8 14.3 %all_to_all.21 = bf16[32,8,128]{2,1,0:T(8,128)(2,1)S(1)} all-to-all(bf16[32,8,128]{2,1,0:T(8,128)(2,1)S(1)} %bitcast.22), channel_id=1, replica_groups=mesh['gxc'=8,'core'=2,'gyh'=4,'gyl'=2,'gz'=2] {'gz','gxc','core'}, dimensions={0} | all-to-all | bytes 131072 | tf_op jit(solution)/shard_map/all_to_all | solution.py:416
  36.1 0.5 shard_map.155
  36.6 0.5 collective-permute-start.6
  37.1 1.4 %shard_map.156 = f32[8,3,8,16,128]{4,3,2,1,0:T(8,128)} custom-call(f32[1,8]{1,0:T(1,128)S(1)} %get-tuple-element.60.decay_ref, f32[1,8]{1,0:T(1,128)S(1)} %get-tuple-element.61.gain_ref, f32[8,3,8,16,128]{4,3,2,1,0:T(8,128)S(1)} %get-tuple-element.62.poles_ref, f32[3,8,16,128]{3,2,1,0:T(8,128)S(1)} %get-tuple-element.74.drive_ref), custom_call_target="tpu_custom_call" | custom-call | bytes 3400000 | tf_op jit(solution)/shard_map/pallas_call | solution.py:417
  38.5 0.4 shard_map.157
  38.9 9.3 %all_to_all.22.got_ref = f32[16,32,128]{2,1,0:T(8,128)S(1)} all-to-all(f32[16,32,128]{2,1,0:T(8,128)S(1)} %shard_map.157), channel_id=1, replica_groups=mesh['gxc'=8,'core'=2,'gyh'=4,'gyl'=2,'gz'=2] {'gxc','gyl'}, dimensions={0} | all-to-all | bytes 524288 | tf_op jit(solution)/shard_map/all_to_all | solution.py:437
  48.3 1.4 %collective-permute-start.7 = (f32[32,128]{1,0:T(8,128)S(1)}, f32[32,128]{1,0:T(8,128)S(1)}, u32[]{:S(2)}, u32[]{:S(2)}) collective-permute-start(f32[32,128]{1,0:T(8,128)S(1)} %shard_map.158.mine_ref), channel_id=1, source_target_pairs={{0,16},{16,0},{1,17},{17,1},{2,18},{18,2},{3,19},{19,3},{4,20},{20... | collective-permute-start | bytes 49160 | tf_op jit(solution)/shard_map/ppermute | solution.py:439
  49.7 0.8 %shard_map.154 = (f32[3,8,16,128]{3,2,1,0:T(8,128)}, f32[3,8,16,128]{3,2,1,0:T(8,128)}) custom-call(f32[3,8,16,128]{3,2,1,0:T(8,128)S(1)} %get-tuple-element.74.drive_ref, f32[3,8,16,128]{3,2,1,0:T(8,128)S(1)} %get-tuple-element.65.base_ref, f32[8,16,128]{2,1,0:T(8,128)S(1)} %get-tuple-element.66.slope_ref, f32[3,8,16,128]{3,2,1,0:T(8,128)S(1)} %get-tuple-element.70.h_ref), custom_call_target="tpu_custom_call" | custom-call | bytes 1200000 | tf_op jit(solution)/shard_map/pallas_call | solution.py:420
  50.5 0.2 shard_map.159
  50.8 15.0 %all_to_all.23 = f32[64,4,128]{2,1,0:T(4,128)S(1)} all-to-all(f32[64,4,128]{2,1,0:T(4,128)S(1)} %bitcast.21), channel_id=1, replica_groups=mesh['gxc'=8,'core'=2,'gyh'=4,'gyl'=2,'gz'=2] {'gyh','gyl','gxc'}, dimensions={0} | all-to-all | bytes 262144 | tf_op jit(solution)/shard_map/all_to_all | solution.py:444
  65.8 0.7 %shard_map.160 = f32[2,2,2048]{2,1,0:T(2,128)} custom-call(f32[256,128]{1,0:T(8,128)S(1)} %bitcast.19), custom_call_target="tpu_custom_call" | custom-call | bytes 300000 | tf_op jit(solution)/shard_map/pallas_call | solution.py:445
  (16 shorter events, 0.5 us)
Async XLA Ops:
  1.7 13.0 %collective-permute-start.1 = (f32[2,32,128]{2,1,0:T(8,128)S(1)}, f32[2,32,128]{2,1,0:T(8,128)S(1)}, u32[]{:S(2)}, u32[]{:S(2)}) collective-permute-start(f32[2,32,128]{2,1,0:T(8,128)S(1)} %get-tuple-element.51), channel_id=1, source_target_pairs={{0,14},{2,0},{4,2},{6,4},{8,6},{10,8},{12,10},{14,12},{1,15},{3,1}... | collective-permute-start | bytes 98312 | tf_op jit(solution)/shard_map/ppermute | solution.py:346
  8.2 6.5 %collective-permute-start.2 = (f32[2,24,128]{2,1,0:T(8,128)S(1)}, f32[2,24,128]{2,1,0:T(8,128)S(1)}, u32[]{:S(2)}, u32[]{:S(2)}) collective-permute-start(f32[2,24,128]{2,1,0:T(8,128)S(1)} %get-tuple-element.52), channel_id=1, source_target_pairs={{1,0},{0,129},{33,32},{32,161},{65,64},{64,193},{97,96},{96,225},{... | collective-permute-start | bytes 73736 | tf_op jit(solution)/shard_map/ppermute | solution.py:379
  10.9 3.8 %collective-permute-start = (f32[2,16,128]{2,1,0:T(8,128)S(1)}, f32[2,16,128]{2,1,0:T(8,128)S(1)}, u32[]{:S(2)}, u32[]{:S(2)}) collective-permute-start(f32[2,16,128]{2,1,0:T(8,128)S(1)} %get-tuple-element.50), channel_id=1, source_target_pairs={{0,240},{16,0},{32,16},{48,32},{64,48},{80,64},{96,80},{112,96},{1... | collective-permute-start | bytes 49160 | tf_op jit(solution)/shard_map/ppermute | solution.py:346
  14.9 6.4 %collective-permute-start.5 = (f32[2,24,128]{2,1,0:T(8,128)S(1)}, f32[2,24,128]{2,1,0:T(8,128)S(1)}, u32[]{:S(2)}, u32[]{:S(2)}) collective-permute-start(f32[2,24,128]{2,1,0:T(8,128)S(1)} %get-tuple-element.55), channel_id=1, source_target_pairs={{0,1},{1,128},{32,33},{33,160},{64,65},{65,192},{96,97},{97,224},{... | collective-permute-start | bytes 73736 | tf_op jit(solution)/shard_map/ppermute | solution.py:395
  15.2 6.1 %collective-permute-start.3 = (f32[2,16,128]{2,1,0:T(8,128)S(1)}, f32[2,16,128]{2,1,0:T(8,128)S(1)}, u32[]{:S(2)}, u32[]{:S(2)}) collective-permute-start(f32[2,16,128]{2,1,0:T(8,128)S(1)} %get-tuple-element.53), channel_id=1, source_target_pairs={{0,16},{16,32},{32,48},{48,64},{64,80},{80,96},{96,112},{112,128},... | collective-permute-start | bytes 49160 | tf_op jit(solution)/shard_map/ppermute | solution.py:346
  17.6 3.7 %collective-permute-start.4 = (f32[2,8,128]{2,1,0:T(8,128)S(1)}, f32[2,8,128]{2,1,0:T(8,128)S(1)}, u32[]{:S(2)}, u32[]{:S(2)}) collective-permute-start(f32[2,8,128]{2,1,0:T(8,128)S(1)} %get-tuple-element.54), channel_id=1, source_target_pairs={{0,2},{2,4},{4,6},{6,8},{8,10},{10,12},{12,14},{14,0},{1,3},{3,5},... | collective-permute-start | bytes 24584 | tf_op jit(solution)/shard_map/ppermute | solution.py:346
  17.8 18.3 %copy-start = (bf16[4,128,2048]{2,1,0:T(8,128)(2,1)S(1)}, bf16[4,128,2048]{2,1,0:T(8,128)(2,1)}, u32[]{:S(2)}) copy-start(bf16[4,128,2048]{2,1,0:T(8,128)(2,1)} %param.22) | copy-start | bytes 6291460
  36.6 1.9 %collective-permute-start.6 = (f32[16,32,128]{2,1,0:T(8,128)S(1)}, f32[16,32,128]{2,1,0:T(8,128)S(1)}, u32[]{:S(2)}, u32[]{:S(2)}) collective-permute-start(f32[16,32,128]{2,1,0:T(8,128)S(1)} %get-tuple-element.83), channel_id=1, source_target_pairs={{0,16},{16,0},{1,17},{17,1},{2,18},{18,2},{3,19},{19,3},{4,20},{20... | collective-permute-start | bytes 786440 | tf_op jit(solution)/shard_map/ppermute | solution.py:432
  38.5 12.0 %copy-start.1 = (bf16[2,256,192]{2,1,0:T(8,128)(2,1)S(1)}, bf16[2,256,192]{2,1,0:T(8,128)(2,1)}, u32[]{:S(2)}) copy-start(bf16[2,256,192]{2,1,0:T(8,128)(2,1)} %constant.33.clone.table_ref) | copy-start | bytes 589828
  48.3 2.2 %collective-permute-start.7 = (f32[32,128]{1,0:T(8,128)S(1)}, f32[32,128]{1,0:T(8,128)S(1)}, u32[]{:S(2)}, u32[]{:S(2)}) collective-permute-start(f32[32,128]{1,0:T(8,128)S(1)} %shard_map.158.mine_ref), channel_id=1, source_target_pairs={{0,16},{16,0},{1,17},{17,1},{2,18},{18,2},{3,19},{19,3},{4,20},{20... | collective-permute-start | bytes 49160 | tf_op jit(solution)/shard_map/ppermute | solution.py:439
